TPU v7x, 256 devices: a whole 4x4x8 slice. The times are simulated.
256 devices in a mesh: dp: 16 (over x_hi, y, core), vocab: 16 (over z, x_lo).
Axes of the slice: x: 4 (x_hi: 2, x_lo: 2; x = x_hi * 2 + x_lo), y: 4, z: 8, core: 2. Of those that a mesh axis runs over, the one named last changes fastest.
Arguments:
- hidden: bfloat16 [512, 4096], P('dp'), may hold values from -6 to 6
- head_weight: bfloat16 [4096, 98304], P(None, ('dp', 'vocab')), may hold values from -0.09375 to 0.09375
- vocab_bias: float32 [98304], P(('dp', 'vocab')), may hold values from -4.5 to 0
- seq_ids: int32 [16, 32], P('dp'), may hold values from 0 to 3, never falling along the last dimension, each value on 1 to 16 neighbouring positions
- token_mask: int32 [16, 32], P('dp'), may hold values 0 or 1
- labels: int32 [32], replicated, may hold values from 0 to 31
Outputs:
- batch_loss: float32 [], replicated
- weight_grad: bfloat16 [4096, 98304], P(None, ('dp', 'vocab'))
- hidden_grad: float32 [512, 4096], P(('dp', 'vocab'))
All inputs are finite; a program needn't handle non-finite values. No bound on the sum of `token_mask` on one device may be relied on, other than what follows from the above.
Results may differ from a plain program's by a relative error of at most 0.011.
Values may be sent and summed in bfloat16 or wider, within the bound.
A program may use at most 128 MiB of HBM per device.

v0:
```python
import jax
import jax.numpy as jnp
from jax import lax
from jax.sharding import PartitionSpec as P

QRY_GROUP = 2
PAS_GROUP = 2
SEQ_GROUP = 4


pool_power = 4.0
score_scale = 20.0
loss_scale = 65536.0
norm_eps = 1e-06
precise = lax.Precision.HIGHEST


def pool_tables(seq_tags, mask_tags):
    groups = seq_tags.shape[0]
    seq_total = groups * SEQ_GROUP
    numbers = (seq_tags + SEQ_GROUP * jnp.arange(groups, dtype=jnp.int32)[:, None]).reshape(-1)
    member = (numbers[None, :] == jnp.arange(seq_total, dtype=jnp.int32)[:, None]) & (
        mask_tags.reshape(-1)[None, :] > 0
    )
    counts = jnp.sum(member.astype(jnp.int32), axis=1)
    return member.astype(jnp.float32) / jnp.maximum(counts, 1).astype(jnp.float32)[:, None]


def split_sequences(pooled):
    groups = pooled.shape[0] // SEQ_GROUP
    shaped = pooled.reshape(groups, SEQ_GROUP, pooled.shape[1])
    return (
        shaped[:, :QRY_GROUP].reshape(-1, pooled.shape[1]),
        shaped[:, QRY_GROUP:].reshape(-1, pooled.shape[1]),
    )


def join_sequences(query_part, passage_part):
    groups = query_part.shape[0] // QRY_GROUP
    feature_width = query_part.shape[1]
    joined = jnp.concatenate(
        (
            query_part.reshape(groups, QRY_GROUP, feature_width),
            passage_part.reshape(groups, PAS_GROUP, feature_width),
        ),
        axis=1,
    )
    return joined.reshape(-1, feature_width)


def products(former, latter):
    return lax.dot_general(
        former,
        latter,
        (((1,), (1,)), ((), ())),
        precision=precise,
        preferred_element_type=jnp.float32,
    )


def project(source, head_weight):
    return lax.dot_general(
        source, head_weight, (((1,), (1,)), ((), ())), preferred_element_type=jnp.float32
    )


def body(hidden, head_weight, vocab_bias, seq_ids, token_mask, labels):
    seq_tags, mask_tags = (
        lax.all_gather(seq_ids, "dp", axis=0, tiled=True),
        lax.all_gather(token_mask, "dp", axis=0, tiled=True),
    )
    pool_weights = pool_tables(seq_tags, mask_tags)
    hidden_all = lax.all_gather(hidden, "dp", axis=0, tiled=True)
    raw_logits = jnp.dot(hidden_all, head_weight, preferred_element_type=jnp.float32)
    logits = raw_logits + vocab_bias[None, :]
    soft_plus = jax.nn.softplus(logits)
    saturated = jnp.log1p(soft_plus)
    excess = (1.0 + saturated) ** pool_power - 1.0
    pooled_sum = jnp.dot(
        pool_weights, excess, precision=precise, preferred_element_type=jnp.float32
    )
    pooled = jnp.log1p(pooled_sum) / pool_power
    query_vecs, passage_vecs = split_sequences(pooled)
    local_squares = jnp.sum(pooled * pooled, axis=1)
    squares = lax.psum(local_squares, ("dp", "vocab"))
    seq_norms = jnp.sqrt(squares + norm_eps)
    query_norms, passage_norms = split_sequences(seq_norms[:, None])
    query_unit = query_vecs / query_norms
    passage_unit = passage_vecs / passage_norms
    cosine = lax.psum(products(query_unit, passage_unit), ("dp", "vocab"))
    scores = score_scale * cosine
    exp_scores = jnp.exp(scores)
    totals = jnp.sum(exp_scores, axis=0)
    chosen = (jnp.arange(scores.shape[0], dtype=jnp.int32)[:, None] == labels[None, :]).astype(
        jnp.float32
    )
    batch_loss = jnp.mean(jnp.log(totals) - jnp.sum(chosen * scores, axis=0))
    score_grad = (
        loss_scale * score_scale / scores.shape[1] * (exp_scores / totals[None, :] - chosen)
    )
    query_dir = jnp.dot(
        score_grad, passage_unit, precision=precise, preferred_element_type=jnp.float32
    )
    passage_dir = lax.dot_general(
        score_grad,
        query_unit,
        (((0,), (0,)), ((), ())),
        precision=precise,
        preferred_element_type=jnp.float32,
    )
    query_radial, passage_radial = lax.psum(
        (jnp.sum(query_unit * query_dir, axis=1), jnp.sum(passage_unit * passage_dir, axis=1)),
        ("dp", "vocab"),
    )
    query_grad = (query_dir - query_unit * query_radial[:, None]) / query_norms
    passage_grad = (passage_dir - passage_unit * passage_radial[:, None]) / passage_norms
    pooled_grad = join_sequences(query_grad, passage_grad)
    sum_grad = pooled_grad / (pool_power * (1.0 + pooled_sum))
    excess_grad = lax.dot_general(
        pool_weights,
        sum_grad,
        (((0,), (0,)), ((), ())),
        precision=precise,
        preferred_element_type=jnp.float32,
    )
    logit_grad = (
        excess_grad
        * pool_power
        * (1.0 + saturated) ** (pool_power - 1.0)
        * jax.nn.sigmoid(logits)
        / (1.0 + soft_plus)
    ).astype(jnp.bfloat16)
    weight_grad = lax.dot_general(
        hidden_all, logit_grad, (((0,), (0,)), ((), ())), preferred_element_type=jnp.float32
    )
    weight_grad = weight_grad.astype(jnp.bfloat16)
    hidden_grad = lax.psum_scatter(
        project(logit_grad, head_weight), ("dp", "vocab"), scatter_dimension=0, tiled=True
    )
    return (batch_loss, weight_grad, hidden_grad)


def solution(mesh):
    in_specs = (
        P("dp", None),
        P(None, ("dp", "vocab")),
        P(("dp", "vocab")),
        P("dp", None),
        P("dp", None),
        P(),
    )
    out_specs = (P(), P(None, ("dp", "vocab")), P(("dp", "vocab"), None))
    return jax.shard_map(body, mesh=mesh, in_specs=in_specs, out_specs=out_specs, check_vma=False)
```

profile of v0, /device:TPU:1, one launch (start us, length us, event | category | flops | bytes accessed | tf_op | source)
XLA Modules:
  0.0 599.3 jit_solution(1635944100072635073)
XLA Ops:
  7.2 0.0 all-gather.4.cloned.1.call-start
  7.2 0.7 all-gather.4.cloned.1.call-update
  7.9 0.0 all-reduce.4.cloned.1.call-start
  8.0 25.9 %all-gather = s32[16,1,32]{2,1,0:T(1,128)S(1)} all-gather(s32[1,1,32]{2,1,0:T(1,128)} %bitcast.22), channel_id=1, replica_groups=mesh['dp'=16,'vocab'=16] {'dp'}, dimensions={0}, use_global_device_ids=true | all-gather | bytes 2176 | tf_op jit(solution)/shard_map/all_gather | solution.py:69
  33.9 0.1 broadcast_add_fusion
  33.9 0.1 eq.28
  34.0 19.3 %all-gather.1 = s32[16,1,32]{2,1,0:T(1,128)S(1)} all-gather(s32[1,1,32]{2,1,0:T(1,128)} %bitcast.23), channel_id=1, replica_groups=mesh['dp'=16,'vocab'=16] {'dp'}, dimensions={0}, use_global_device_ids=true | all-gather | bytes 2176 | tf_op jit(solution)/shard_map/all_gather | solution.py:70
  53.3 0.1 gt.16
  53.4 0.1 convert_reduce_fusion
  53.6 21.8 %all-gather.4.cloned.1.call-done = bf16[512,4096]{1,0:T(8,128)(2,1)} async-done(((bf16[32,4096]{1,0:T(8,128)(2,1)}), bf16[512,4096]{1,0:T(8,128)(2,1)}) %all-gather.4.cloned.1.call-update) | async-done | bytes 4194320 | tf_op jit(solution)/shard_map/all_gather | solution.py:73
  75.3 4.6 convolution_add_fusion
  79.9 2.1 log-plus-one_multiply_fusion
  82.1 74.9 %psum.28 = f32[64]{0:T(128)S(1)} all-reduce(f32[64]{0:T(128)S(1)} %get-tuple-element.24), channel_id=1, replica_groups=mesh['dp'=16,'vocab'=16] {'dp','vocab'}, use_global_device_ids=true, to_apply=%region_2.3 | all-reduce | flops 64 | bytes 512 | tf_op jit(solution)/shard_map/psum | solution.py:85
  157.0 0.1 reshape_broadcast_in_dim.3
  157.1 0.1 fusion.37
  157.2 0.1 fusion.36
  157.4 0.2 fusion.38
  157.6 73.8 %psum.29 = f32[32,32]{1,0:T(8,128)S(1)} all-reduce(f32[32,32]{1,0:T(8,128)S(1)} %fusion.38), channel_id=1, replica_groups=mesh['dp'=16,'vocab'=16] {'dp','vocab'}, use_global_device_ids=true, to_apply=%region_3.4 | all-reduce | flops 1024 | bytes 8192 | tf_op jit(solution)/shard_map/psum | solution.py:90
  231.4 0.1 div.95
  231.6 0.1 div.98
  231.7 0.4 multiply_reduce_fusion.1
  232.1 0.4 multiply_reduce_fusion.2
  232.4 73.6 %all-reduce.1 = (f32[32]{0:T(128)S(1)}, f32[32]{0:T(128)S(1)}) all-reduce(f32[32]{0:T(128)S(1)} %get-tuple-element.30, f32[32]{0:T(128)S(1)} %get-tuple-element.32), channel_id=1, replica_groups=mesh['dp'=16,'vocab'=16] {'dp','vocab'}, use_global_device_ids=true, to_apply=%region_10.11 | all-reduce | flops 64 | bytes 512 | tf_op jit(solution)/shard_map/psum | solution.py:111
  306.0 0.1 subtract_divide_fusion
  306.2 0.7 reshape.69
  306.9 3.0 fusion.4
  309.9 5.6 fusion.39
  315.5 5.7 fusion
  321.2 4.7 copy.28
  325.9 0.6 subtract_reduce_fusion
  327.2 262.6 %all-reduce.4.cloned.1.call-done = f32[512,4096]{1,0:T(8,128)} async-done(((f32[512,4096]{1,0:T(8,128)}), f32[512,4096]{1,0:T(8,128)}) %all-reduce.4.cloned.1.call-update) | async-done | bytes 8388624
  589.8 1.5 constant_dynamic-slice_fusion
  (22 shorter events, 0.4 us)
Async XLA Ops:
  7.2 68.2 %copy-start = (bf16[4096,384]{1,0:T(8,128)(2,1)S(1)}, bf16[4096,384]{1,0:T(8,128)(2,1)}, u32[]{:S(2)}) copy-start(bf16[4096,384]{1,0:T(8,128)(2,1)} %param.7) | copy-start | bytes 9437188
  7.2 68.2 %all-gather.4.cloned.1.call-start = ((), (), s32[]{:S(2)}) async-start(), calls=%async_computation | async-start | bytes 4456448 | tf_op jit(solution)/shard_map/all_gather | solution.py:73
  7.9 581.8 %all-reduce.4.cloned.1.call-start = ((), (), s32[]{:S(2)}) async-start(), calls=%async_computation.1 | async-start | bytes 16777216
  53.5 26.4 %copy-start.2 = (f32[64]{0:T(128)}, f32[64]{0:T(128)S(1)}, u32[]{:S(2)}) copy-start(f32[64]{0:T(128)S(1)} %maximum_convert_fusion) | copy-start | bytes 772
  79.9 2.1 copy-start.3
  79.9 151.7 %copy-start.1 = (s32[32]{0:T(128)S(1)}, s32[32]{0:T(128)}, u32[]{:S(2)}) copy-start(s32[32]{0:T(128)} %param.11) | copy-start | bytes 388
Sparse Core Ops, SparseCore 0:
  10.8 64.5 all-gather.3
  315.6 274.0 all-reduce.3
where the time goes:
time: 600 us; the launch traced here: 599 us
  waiting for transfers between devices  285 us (48%)
  blocking collectives  267 us (44%)
  matrix products  21.8 us (4%)
  between operations  16 us (3%)
  local copies, waits for them, and re-layouts  7.64 us (1%)
    unnamed x3, waiting for transfers between devices  263 us
    psum x1, blocking collectives, body(): squares = lax.psum(local_squares, ('dp', 'vocab'))  74.9 us
    psum x1, blocking collectives, body(): cosine = lax.psum(products(query_unit, passage_unit), ('dp', 'vocab'))  73.8 us
    psum x1, blocking collectives, body(): lax.psum((jnp.sum(query_unit * query_dir, axis=1), jnp.sum(passage_unit *...  73.6 us
    all_gather x1, blocking collectives, body(): lax.all_gather(seq_ids, 'dp', axis=0, tiled=True)  25.9 us
    all_gather x1, waiting for transfers between devices, body(): hidden_all = lax.all_gather(hidden, 'dp', axis=0, tiled=True)  21.8 us
    all_gather x1, blocking collectives, body(): lax.all_gather(token_mask, 'dp', axis=0, tiled=True)  19.3 us
  transfers between devices with their start and end apart: 2, of which 2 were waited for; matrix products, arithmetic and copies ran while one was open for 2% of the time, Pallas kernels for 0%

commit v1 on v0

v1 whole, which is shorter than its diff:
```python
import functools

import jax
import jax.numpy as jnp
from jax import lax
from jax.experimental import pallas as pl
from jax.experimental.pallas import tpu as pltpu
from jax.sharding import PartitionSpec as P

MESH = pl.DeviceIdType.MESH
F32, BF16 = jnp.float32, jnp.bfloat16

SEQ_GROUP = 4
GROUPS = 16
TOK = 32
SIDE = 4
DEPTH = 8
TAG = 128

score_scale = 20.0
loss_scale = 65536.0
norm_eps = 1e-06
precise = lax.Precision.HIGHEST

GATHER_COPIES = 24
PAIR = 16


def iota(shape, dim):
    return lax.broadcasted_iota(jnp.int32, shape, dim)


def split3(x):
    first = x.astype(BF16)
    rest = x - first.astype(F32)
    second = rest.astype(BF16)
    third = (rest - second.astype(F32)).astype(BF16)
    return first, second, third


def dot(a, b, dims=((1,), (0,)), precision=None):
    return lax.dot_general(a, b, (dims, ((), ())), precision=precision, preferred_element_type=F32)


def fused(
    hidden_ref, weight_ref, bias_ref, seq_ref, mask_ref, labels_ref,
    loss_ref, wgrad_ref, hgrad_ref,
    hid, w, wsib, logit, fac, excess, mt, lg, lgp, lgs,
    ara, arb, part, farl, farr, fromm, fromp, acc, rtwo, zsend, zrecv, wg,
    loc_sem, g_send, g_recv, e_send, e_recv, a_send, a_recv, b_send, b_recv,
    r_send, r_recv, s_send, s_recv, z_send, z_recv,
):
    width = hidden_ref.shape[1]
    half = width // 2
    voc = weight_ref.shape[1]
    d, v = lax.axis_index("dp"), lax.axis_index("vocab")
    core, y, xh = d % 2, (d // 2) % 4, d // 8
    xl, z = v % 2, v // 2
    x = xh * 2 + xl

    def place(px, py, pc, pz):
        return ((px // 2) * 8 + py * 2 + pc, pz * 2 + px % 2)

    def group(gxh, gy, gc):
        return gxh * 8 + gy * 2 + gc

    def column_mate(k):
        return place(x, y, (core + k // DEPTH) % 2, (z + k % DEPTH) % DEPTH)

    def plane_mate(k):
        return place((x + k // SIDE) % SIDE, (y + k % SIDE) % SIDE, core, z)

    def remote(src, dst, send, recv, device):
        return pltpu.make_async_remote_copy(
            src_ref=src, dst_ref=dst, send_sem=send, recv_sem=recv, device_id=device, device_id_type=MESH
        )

    w_copies = [
        pltpu.make_async_copy(weight_ref.at[pl.ds(h * half, half), :], w.at[h], loc_sem.at[h]) for h in range(2)
    ]
    h_copies = [
        pltpu.make_async_copy(
            hidden_ref.at[:, pl.ds(h * half, half)], hid.at[d, h, :, pl.ds(0, half)], loc_sem.at[2 + h]
        )
        for h in range(2)
    ]
    for copy in h_copies + w_copies:
        copy.start()

    barrier = pltpu.get_barrier_semaphore()
    for k in range(1, PAIR):
        pl.semaphore_signal(barrier, inc=1, device_id=column_mate(k), device_id_type=MESH)
        pl.semaphore_signal(barrier, inc=1, device_id=plane_mate(k), device_id_type=MESH)

    tag_row = jnp.where(mask_ref[...] > 0, seq_ref[...], SEQ_GROUP).astype(F32)
    eye = iota((TOK, TOK), 0) == iota((TOK, TOK), 1)
    tag_col = jnp.sum(jnp.where(eye, jnp.broadcast_to(tag_row, (TOK, TOK)), 0.0), axis=1, keepdims=True)
    tag_block = jnp.broadcast_to(tag_col, (TOK, TAG)).astype(BF16)
    for h in range(2):
        hid[d, h, :, pl.ds(half, TAG)] = tag_block
    for copy in h_copies:
        copy.wait()
    pl.semaphore_wait(barrier, 2 * (PAIR - 1))

    up, down = (y + 1) % 4, (y + 3) % 4
    far = (y + 2) % 4
    to_up, to_down = place(x, up, core, z), place(x, down, core, z)
    other = 1 - xh
    to_cross = place(other * 2 + 1 - xl, y, core, z)
    to_twin = place(xh * 2 + 1 - xl, y, core, z)
    to_sib = place(x, y, 1 - core, z)
    sent = []

    def gsend(k, chunk, device):
        copy = remote(chunk, chunk, g_send.at[k], g_recv.at[k], device)
        copy.start()
        sent.append(copy)

    def gwait(k, chunk):
        remote(chunk, chunk, g_send.at[k], g_recv.at[k], to_sib).wait_recv()

    own = hid.at[d]
    c_down, c_up, c_far = (hid.at[group(xh, yy, core)] for yy in (down, up, far))
    cross_y = (y, down, up, far)

    gsend(0, own, to_up)
    gsend(1, own, to_down)
    gsend(2, hid.at[d, 1 - xl], to_cross)
    gsend(3, own, to_sib)

    def crossed(i, k):
        chunk = hid.at[group(other, cross_y[i], core), xl]
        gwait(k, chunk)
        gsend(12 + i, chunk, to_twin)
        gsend(16 + i, chunk, to_sib)

    crossed(0, 2)
    gwait(0, c_down)
    gsend(4, hid.at[group(xh, down, core), 0], to_up)
    gsend(5, hid.at[group(xh, down, core), 1 - xl], to_cross)
    gsend(6, c_down, to_sib)
    gwait(1, c_up)
    gsend(7, hid.at[group(xh, up, core), 1], to_down)
    gsend(8, hid.at[group(xh, up, core), 1 - xl], to_cross)
    gsend(9, c_up, to_sib)
    gwait(4, hid.at[group(xh, far, core), 0])
    gwait(7, hid.at[group(xh, far, core), 1])
    gsend(10, hid.at[group(xh, far, core), 1 - xl], to_cross)
    gsend(11, c_far, to_sib)
    crossed(1, 5)
    crossed(2, 8)
    crossed(3, 10)
    for i in range(4):
        chunk = hid.at[group(other, cross_y[i], core), 1 - xl]
        gwait(12 + i, chunk)
        gsend(20 + i, chunk, to_sib)

    for copy in w_copies:
        copy.wait()
    w_swap = remote(w.at[1 - core], wsib, e_send.at[0], e_recv.at[0], to_sib)
    w_swap.start()

    gwait(3, hid.at[group(xh, y, 1 - core)])
    gwait(6, hid.at[group(xh, down, 1 - core)])
    gwait(9, hid.at[group(xh, up, 1 - core)])
    gwait(11, hid.at[group(xh, far, 1 - core)])
    for i in range(4):
        gwait(16 + i, hid.at[group(other, cross_y[i], 1 - core), xl])
        gwait(20 + i, hid.at[group(other, cross_y[i], 1 - core), 1 - xl])

    tokens = GROUPS * TOK
    deep = min(512, half)
    per_half = half // deep

    logit[...] = jnp.broadcast_to(bias_ref[...], (tokens, voc))

    def logit_step(i, carry):
        h = i // per_half
        start = pl.multiple_of((i % per_half) * deep, deep)
        a = hid[:, h, :, pl.ds(start, deep)].reshape(tokens, deep)
        logit[...] += dot(a, w[h, pl.ds(start, deep), :])
        return carry

    lax.fori_loop(0, 2 * per_half, logit_step, 0)

    tags = hid[:, 0, :, pl.ds(half, TAG)].reshape(tokens, TAG).astype(F32)
    lane = iota((tokens, TAG), 1)
    index = lane % 32
    wanted_group = index // 2
    wanted_tag = index % 2 + 2 * (lane // 32)
    belongs = (
        (iota((tokens, TAG), 0) // TOK == wanted_group)
        & (tags == wanted_tag.astype(F32))
        & (tags < SEQ_GROUP)
        & (lane < 64)
    )
    member_t = jnp.where(belongs, 1.0, 0.0)
    mt[...] = member_t.astype(BF16)
    member = jnp.transpose(member_t)
    inv_count = 1.0 / jnp.maximum(jnp.sum(member, axis=1, keepdims=True), 1.0)
    member = member.astype(BF16)

    def excess_step(i, carry):
        rows = pl.ds(pl.multiple_of(i * TOK, TOK), TOK)
        l = logit[rows, :]
        soft = jnp.maximum(l, 0.0) + jnp.log1p(jnp.exp(-jnp.abs(l)))
        u = 1.0 + jnp.log1p(soft)
        u2 = u * u
        excess[rows, :] = u2 * u2 - 1.0
        return carry

    lax.fori_loop(0, GROUPS, excess_step, 0)
    e1, e2, e3 = split3(excess[...])
    pooled_sum = (dot(member, e1) + dot(member, e2) + dot(member, e3)) * inv_count
    pooled = jnp.log1p(pooled_sum) * 0.25

    wide = iota((32, TAG), 1)
    in_passages = (wide >= 32) & (wide < 64)
    inner = dot(pooled[:32], pooled, ((1,), (1,)), precise)
    inner = jnp.where(in_passages, inner, 0.0)
    packed = inner[0:8]
    packed = pltpu.roll(packed, 96, 1)
    for b in range(1, 4):
        shift = 32 * (b - 1)
        piece = inner[8 * b : 8 * b + 8]
        packed = packed + (pltpu.roll(piece, shift, 1) if shift else piece)
    squares = dot(jnp.ones((8, voc), F32), pooled * pooled, ((1,), (1,)), precise)

    slot = core * DEPTH + z
    ara[slot, 0:8, :] = packed
    ara[slot, 8:16, :] = squares
    a_copies = [
        remote(ara.at[slot], ara.at[slot], a_send.at[k], a_recv.at[k], column_mate(k)) for k in range(1, PAIR)
    ]
    for copy in a_copies:
        copy.start()

    def factor_step(i, carry):
        rows = pl.ds(pl.multiple_of(i * TOK, TOK), TOK)
        l = logit[rows, :]
        e = jnp.exp(-jnp.abs(l))
        soft = jnp.maximum(l, 0.0) + jnp.log1p(e)
        u = 1.0 + jnp.log1p(soft)
        top = jnp.where(l >= 0.0, 1.0, e)
        fac[rows, :] = 4.0 * (u * u * u) * top / ((1.0 + e) * (1.0 + soft))
        return carry

    lax.fori_loop(0, GROUPS, factor_step, 0)

    for copy in a_copies:
        copy.wait_recv()
    column_sum = ara[0]
    for k in range(1, PAIR):
        column_sum = column_sum + ara[k]
    slot_b = x * SIDE + y
    arb[slot_b] = column_sum
    b_copies = [
        remote(arb.at[slot_b], arb.at[slot_b], b_send.at[k], b_recv.at[k], plane_mate(k)) for k in range(1, PAIR)
    ]
    for copy in b_copies:
        copy.start()
    for copy in b_copies:
        copy.wait_recv()
    total = arb[0]
    for k in range(1, PAIR):
        total = total + arb[k]

    pieces = []
    for b in range(4):
        shift = (32 - 32 * b) % 128
        pieces.append(pltpu.roll(total[0:8], shift, 1) if shift else total[0:8])
    inner = jnp.where(in_passages, jnp.concatenate(pieces, axis=0), 0.0)
    square_row = total[8:9]
    eye_wide = iota((TAG, TAG), 0) == iota((TAG, TAG), 1)
    square_col = jnp.sum(jnp.where(eye_wide, jnp.broadcast_to(square_row, (TAG, TAG)), 0.0), axis=1, keepdims=True)
    norm_row = jnp.sqrt(square_row + norm_eps)
    norm_col = jnp.sqrt(square_col + norm_eps)
    cosine = inner / (norm_col[:32] * norm_row)
    scores = score_scale * cosine
    exp_scores = jnp.where(in_passages, jnp.exp(scores), 0.0)
    totals = jnp.sum(exp_scores, axis=0, keepdims=True)
    totals = jnp.where(in_passages[0:1], totals, 1.0)
    labels = labels_ref[...].astype(F32)
    label_col = jnp.sum(jnp.where(eye, jnp.broadcast_to(labels, (32, 32)), 0.0), axis=1, keepdims=True)
    row_id = iota((32, TAG), 0)
    label_row = jnp.sum(
        jnp.where(wide - 32 == row_id, jnp.broadcast_to(label_col, (32, TAG)), 0.0), axis=0, keepdims=True
    )
    chosen = jnp.where((row_id.astype(F32) == label_row) & in_passages, 1.0, 0.0)
    per_passage = jnp.log(totals) - jnp.sum(chosen * scores, axis=0, keepdims=True)
    loss_ref[...] = jnp.sum(per_passage, axis=1, keepdims=True) / 32.0
    score_grad = (loss_scale * score_scale / 32.0) * (exp_scores / totals - chosen)
    blank = jnp.zeros((TAG - 32, TAG), F32)
    grad_full = jnp.concatenate([score_grad, blank], axis=0)
    cos_full = jnp.concatenate([cosine, blank], axis=0)
    grad_sym = grad_full + jnp.transpose(grad_full)
    cos_sym = cos_full + jnp.transpose(cos_full)
    radial = jnp.sum(grad_sym * cos_sym, axis=1, keepdims=True)
    inv_norm = 1.0 / norm_col
    unit = pooled * inv_norm
    pooled_grad = (dot(grad_sym, unit, precision=precise) - unit * radial) * inv_norm
    sum_grad = pooled_grad * inv_count / (4.0 * (1.0 + pooled_sum))

    s1, s2, s3 = split3(sum_grad)
    new, old = iota((64, 64), 0), iota((64, 64), 1)
    source = ((new // 16) % 2) * 32 + ((new // 2) % 8) * 4 + (new // 32) * 2 + new % 2
    shuffle = jnp.where(source == old, 1.0, 0.0).astype(BF16)

    def grad_step(i, carry):
        rows = pl.ds(pl.multiple_of(i * 64, 64), 64)
        m = mt[rows, :]
        g = (dot(m, s1) + dot(m, s2) + dot(m, s3)) * fac[rows, :]
        g = g.astype(BF16)
        lg[rows, :] = g
        p = dot(shuffle, g).astype(BF16)
        lgp[(i // 4) * 2, i % 4] = p[:32]
        lgp[(i // 4) * 2 + 1, i % 4] = p[32:]
        return carry

    lax.fori_loop(0, 8, grad_step, 0)
    lg_swap = remote(lgp, lgs, e_send.at[1], e_recv.at[1], to_sib)
    lg_swap.start()
    w_swap.wait_recv()
    lg_swap.wait_recv()

    block = min(512, half)

    def partial(o):
        def rows_of(ref):
            picked = []
            for i in range(4):
                px = (1 - core) * ((x + o) % 4) + core * i
                py = core * ((y + o) % 4) + (1 - core) * i
                picked.append(ref[px, py])
            return jnp.concatenate(picked, axis=0)

        mine, theirs = rows_of(lgp), rows_of(lgs)

        def step(n, carry):
            start = pl.multiple_of(n * block, block)
            cols = pl.ds(start, block)
            value = dot(mine, w[core, cols, :], ((1,), (1,))) + dot(theirs, wsib[cols, :], ((1,), (1,)))
            part[o, :, :, cols] = value.astype(BF16).reshape(4, 32, block)
            return carry

        lax.fori_loop(0, half // block, step, 0)

    quarter = half // 2
    left, right = pl.ds(0, quarter), pl.ds(quarter, quarter)

    def ring(o):
        return place((x + (1 - core) * o) % 4, (y + core * o) % 4, core, z)

    def ring_two(o):
        return place((x + core * o) % 4, (y + (1 - core) * o) % 4, core, z)

    plus, minus = ring(1), ring(3)
    partial(2)
    far_l = remote(part.at[2, :, :, left], farl, r_send.at[0], r_recv.at[0], plus)
    far_r = remote(part.at[2, :, :, right], farr, r_send.at[1], r_recv.at[1], minus)
    far_l.start()
    far_r.start()
    partial(1)
    plain_r = remote(part.at[1, :, :, right], fromm.at[1], r_send.at[2], r_recv.at[2], plus)
    plain_r.start()
    partial(3)
    plain_l = remote(part.at[3, :, :, left], fromp.at[0], r_send.at[3], r_recv.at[3], minus)
    plain_l.start()
    partial(0)
    far_l.wait_recv()
    part[1, :, :, left] = (part[1, :, :, left].astype(F32) + farl[...].astype(F32)).astype(BF16)
    sum_l = remote(part.at[1, :, :, left], fromm.at[0], r_send.at[4], r_recv.at[4], plus)
    sum_l.start()
    far_r.wait_recv()
    part[3, :, :, right] = (part[3, :, :, right].astype(F32) + farr[...].astype(F32)).astype(BF16)
    sum_r = remote(part.at[3, :, :, right], fromp.at[1], r_send.at[5], r_recv.at[5], minus)
    sum_r.start()

    def weight_step(i, carry):
        h = i // per_half
        start = pl.multiple_of((i % per_half) * deep, deep)
        a = hid[:, h, :, pl.ds(start, deep)].reshape(tokens, deep)
        wg[h, pl.ds(start, deep), :] = dot(a, lg[...], ((0,), (0,))).astype(BF16)
        return carry

    lax.fori_loop(0, 2 * per_half, weight_step, 0)
    wg_copies = [
        pltpu.make_async_copy(wg.at[h], wgrad_ref.at[pl.ds(h * half, half), :], loc_sem.at[4 + h]) for h in range(2)
    ]
    for copy in wg_copies:
        copy.start()

    for copy in (plain_r, plain_l, sum_l, sum_r):
        copy.wait_recv()
    for h, cols in ((0, left), (1, right)):
        value = part[0, :, :, cols].astype(F32) + fromm[h].astype(F32) + fromp[h].astype(F32)
        acc[:, :, cols] = value.astype(BF16)

    seat = core * x + (1 - core) * y
    two_copies = [
        remote(acc.at[(seat + o) % 4], rtwo.at[o - 1], s_send.at[o - 1], s_recv.at[o - 1], ring_two(o))
        for o in range(1, 4)
    ]
    for copy in two_copies:
        copy.start()
    for copy in two_copies:
        copy.wait_recv()
    rows = acc[seat].astype(F32)
    for o in range(3):
        rows = rows + rtwo[o].astype(F32)
    rows = rows.astype(BF16)

    slab = half // 8
    stacked = jnp.concatenate([rows[:, b * slab : (b + 1) * slab] for b in range(8)], axis=0)
    new, old = iota((256, 256), 0), iota((256, 256), 1)
    source = (new % 8) * 32 + (new // 16) * 2 + (new // 8) % 2
    shuffle = jnp.where(source == old, 1.0, 0.0).astype(BF16)
    zsend[...] = dot(shuffle, stacked).astype(BF16).reshape(16, 16, slab)
    z_copies = []
    for k in range(1, PAIR):
        target = ((core + k // DEPTH) % 2) * DEPTH + (z + k % DEPTH) % DEPTH
        copy = remote(zsend.at[target], zrecv.at[slot], z_send.at[k], z_recv.at[k], column_mate(k))
        copy.start()
        z_copies.append(copy)
    zrecv[slot] = zsend[slot]
    for copy in z_copies:
        copy.wait_recv()
    for c in range(2):
        value = zrecv[c * DEPTH].astype(F32)
        for k in range(1, DEPTH):
            value = value + zrecv[c * DEPTH + k].astype(F32)
        for r in range(2):
            for b in range(8):
                hgrad_ref[r : r + 1, pl.ds(c * half + b * slab, slab)] = value[r * 8 + b : r * 8 + b + 1]

    for copy in sent + [w_swap, lg_swap] + a_copies + b_copies:
        copy.wait_send()
    for copy in [far_l, far_r, plain_r, plain_l, sum_l, sum_r] + two_copies + z_copies:
        copy.wait_send()
    for copy in wg_copies:
        copy.wait()


def body(hidden, head_weight, vocab_bias, seq_ids, token_mask, labels):
    width, voc = head_weight.shape
    half = width // 2
    tokens = GROUPS * TOK
    vmem = pl.BlockSpec(memory_space=pltpu.VMEM)
    hbm = pl.BlockSpec(memory_space=pl.ANY)
    dma = pltpu.SemaphoreType.DMA
    loss, weight_grad, hidden_grad = pl.pallas_call(
        fused,
        out_shape=(
            jax.ShapeDtypeStruct((1, 1), F32),
            jax.ShapeDtypeStruct((width, voc), BF16),
            jax.ShapeDtypeStruct((2, width), F32),
        ),
        in_specs=[hbm, hbm, vmem, vmem, vmem, vmem],
        out_specs=(vmem, hbm, vmem),
        scratch_shapes=[
            pltpu.VMEM((GROUPS, 2, TOK, half + TAG), BF16),
            pltpu.VMEM((2, half, voc), BF16),
            pltpu.VMEM((half, voc), BF16),
            pltpu.VMEM((tokens, voc), F32),
            pltpu.VMEM((tokens, voc), F32),
            pltpu.VMEM((tokens, voc), F32),
            pltpu.VMEM((tokens, TAG), BF16),
            pltpu.VMEM((tokens, voc), BF16),
            pltpu.VMEM((4, 4, TOK, voc), BF16),
            pltpu.VMEM((4, 4, TOK, voc), BF16),
            pltpu.VMEM((PAIR, 16, TAG), F32),
            pltpu.VMEM((PAIR, 16, TAG), F32),
            pltpu.VMEM((4, 4, TOK, half), BF16),
            pltpu.VMEM((4, TOK, half // 2), BF16),
            pltpu.VMEM((4, TOK, half // 2), BF16),
            pltpu.VMEM((2, 4, TOK, half // 2), BF16),
            pltpu.VMEM((2, 4, TOK, half // 2), BF16),
            pltpu.VMEM((4, TOK, half), BF16),
            pltpu.VMEM((3, TOK, half), BF16),
            pltpu.VMEM((PAIR, 16, half // 8), BF16),
            pltpu.VMEM((PAIR, 16, half // 8), BF16),
            pltpu.VMEM((2, half, voc), BF16),
            dma((6,)),
            dma((GATHER_COPIES,)),
            dma((GATHER_COPIES,)),
            dma((2,)),
            dma((2,)),
            dma((PAIR,)),
            dma((PAIR,)),
            dma((PAIR,)),
            dma((PAIR,)),
            dma((6,)),
            dma((6,)),
            dma((3,)),
            dma((3,)),
            dma((PAIR,)),
            dma((PAIR,)),
        ],
        compiler_params=pltpu.CompilerParams(
            collective_id=0, has_side_effects=True, vmem_limit_bytes=48 * 1024 * 1024
        ),
        name="splade_head",
    )(
        hidden,
        head_weight,
        vocab_bias.reshape(1, voc),
        seq_ids,
        token_mask,
        labels.reshape(1, labels.shape[0]),
    )
    return loss.reshape(()), weight_grad, hidden_grad


def solution(mesh):
    in_specs = (
        P("dp", None),
        P(None, ("dp", "vocab")),
        P(("dp", "vocab")),
        P("dp", None),
        P("dp", None),
        P(),
    )
    out_specs = (P(), P(None, ("dp", "vocab")), P(("dp", "vocab"), None))
    return jax.shard_map(body, mesh=mesh, in_specs=in_specs, out_specs=out_specs, check_vma=False)
```

time: 600 us -> 94.1 us (0.16)
  waiting for transfers between devices: 285 us -> 0 us
  blocking collectives: 267 us -> 0 us
  Pallas kernels: 0 us -> 85.7 us
  matrix products: 21.8 us -> 0 us
  between operations: 16 us -> 2.39 us
    unnamed x3 -> x0, waiting for transfers between devices: 263 us -> none
    psum x3 -> x0, blocking collectives: 222 us -> none  [the longest x1 74.9 us: body(): squares = lax.psum(local_squares, ('dp', 'vocab'))]
    pallas_call x0 -> x1, Pallas kernels: none -> 85.7 us  [body(): pl.pallas_call(fused, out_shape=(jax.ShapeDtypeStruct((1, 1), F32), jax.S...]
    all_gather x2 -> x0, blocking collectives: 45.2 us -> none  [the longest x1 25.9 us: body(): lax.all_gather(seq_ids, 'dp', axis=0, tiled=True)]
    dot_general x8 -> x0, matrix products: 21.8 us -> none  [the longest x1 5.69 us: body(): lax.dot_general(hidden_all, logit_grad, (((0,), (0,)), ((), ())), preferr...]
    all_gather x1 -> x0, waiting for transfers between devices: 21.8 us -> none  [body(): hidden_all = lax.all_gather(hidden, 'dp', axis=0, tiled=True)]
  transfers between devices with their start and end apart: 2 -> 0, of which waited for: 2 -> 0; matrix products, arithmetic and copies ran while one was open for 2% -> 0% of each run, Pallas kernels for 0% -> 0%
where the time goes in v1:
time: 94.1 us; the launch traced here: 94 us
  Pallas kernels  85.7 us (91%)
  local copies, waits for them, and re-layouts  5.88 us (6%)
  between operations  2.39 us (3%)
    pallas_call x1, Pallas kernels, body(): pl.pallas_call(fused, out_shape=(jax.ShapeDtypeStruct((1, 1), F32), jax.S...  85.7 us
    unnamed x10, local copies, waits for them, and re-layouts  5.19 us

profile of v1, /device:TPU:1, one launch (start us, length us, event | category | flops | bytes accessed | tf_op | source)
XLA Modules:
  0.0 94.0 jit_solution(3660123569478186310)
XLA Ops:
  0.6 0.7 reshape.15.bias_ref
  1.3 0.0 copy-start
  1.3 0.9 %copy-done = bf16[32,4096]{1,0:T(8,128)(2,1)S(1)} copy-done((bf16[32,4096]{1,0:T(8,128)(2,1)S(1)}, bf16[32,4096]{1,0:T(8,128)(2,1)}, u32[]{:S(2)}) %copy-start) | copy-done | bytes 262168
  2.3 0.0 copy-start.1
  2.3 0.7 copy-done.1
  2.9 0.0 copy-start.2
  2.9 0.7 copy-done.2
  3.6 0.0 copy-start.3
  3.6 0.7 copy-done.3
  4.2 85.7 %splade_head.1 = (f32[1,1]{1,0:T(1,128)}, bf16[4096,384]{1,0:T(8,128)(2,1)S(1)}, f32[2,4096]{1,0:T(2,128)S(1)}) custom-call(bf16[32,4096]{1,0:T(8,128)(2,1)S(1)} %copy-done, bf16[4096,384]{1,0:T(8,128)(2,1)} %weight_ref.1, f32[1,384]{1,0:T(1,128)S(1)} %reshape.15.bias_ref, s32[1,32]{1,0:T(1,128)S(1)} %copy-done.1, s32[1,32]{1,0:T(1,128)S(1)} %copy-done.2, ...), custom_call_target="tpu_custom_call" | custom-call | tf_op jit(solution)/shard_map/splade_head/pallas_call | solution.py:451
  90.6 1.7 %copy.13 = bf16[4096,384]{1,0:T(8,128)(2,1)} copy(bf16[4096,384]{1,0:T(8,128)(2,1)S(1)} %get-tuple-element.13) | data formatting | bytes 6291456
  92.2 0.6 copy.14
Async XLA Ops:
  1.3 0.9 %copy-start = (bf16[32,4096]{1,0:T(8,128)(2,1)S(1)}, bf16[32,4096]{1,0:T(8,128)(2,1)}, u32[]{:S(2)}) copy-start(bf16[32,4096]{1,0:T(8,128)(2,1)} %hidden_ref.1) | copy-start | bytes 786436
  2.3 0.7 copy-start.1
  2.9 0.7 copy-start.2
  3.6 0.7 copy-start.3

commit v2 on v1

--- a/solution.py
+++ b/solution.py
@@ -22,7 +22,7 @@
 norm_eps = 1e-06
 precise = lax.Precision.HIGHEST
 
-GATHER_COPIES = 24
+GATHER_COPIES = 28
 PAIR = 16
 
 
@@ -43,11 +43,11 @@
 
 
 def fused(
-    hidden_ref, weight_ref, bias_ref, seq_ref, mask_ref, labels_ref,
+    hidden_ref, weight_ref, rows_ref,
     loss_ref, wgrad_ref, hgrad_ref,
-    hid, w, wsib, logit, fac, excess, mt, lg, lgp, lgs,
-    ara, arb, part, farl, farr, fromm, fromp, acc, rtwo, zsend, zrecv, wg,
-    loc_sem, g_send, g_recv, e_send, e_recv, a_send, a_recv, b_send, b_recv,
+    hid, tags_ref, w, wsib, logit, fac, excess, mt, lg, lgp, lgs,
+    ara, arb, pre, part, farl, farr, fromm, fromp, acc, rtwo, zsend, zrecv,
+    loc_sem, g_send, g_recv, h_send, h_recv, t_send, t_recv, e_send, e_recv, a_send, a_recv, b_send, b_recv,
     r_send, r_recv, s_send, s_recv, z_send, z_recv,
 ):
     width = hidden_ref.shape[1]
@@ -75,14 +75,18 @@
             src_ref=src, dst_ref=dst, send_sem=send, recv_sem=recv, device_id=device, device_id_type=MESH
         )
 
+    sent = []
+
+    def launch(copy):
+        copy.start()
+        sent.append(copy)
+
     w_copies = [
         pltpu.make_async_copy(weight_ref.at[pl.ds(h * half, half), :], w.at[h], loc_sem.at[h]) for h in range(2)
     ]
+    quad = width // 4
     h_copies = [
-        pltpu.make_async_copy(
-            hidden_ref.at[:, pl.ds(h * half, half)], hid.at[d, h, :, pl.ds(0, half)], loc_sem.at[2 + h]
-        )
-        for h in range(2)
+        pltpu.make_async_copy(hidden_ref.at[:, pl.ds(q * quad, quad)], hid.at[d, q], loc_sem.at[2 + q]) for q in range(4)
     ]
     for copy in h_copies + w_copies:
         copy.start()
@@ -92,98 +96,106 @@
         pl.semaphore_signal(barrier, inc=1, device_id=column_mate(k), device_id_type=MESH)
         pl.semaphore_signal(barrier, inc=1, device_id=plane_mate(k), device_id_type=MESH)
 
-    tag_row = jnp.where(mask_ref[...] > 0, seq_ref[...], SEQ_GROUP).astype(F32)
     eye = iota((TOK, TOK), 0) == iota((TOK, TOK), 1)
+    tag_row = rows_ref[2:3, 0:TOK]
     tag_col = jnp.sum(jnp.where(eye, jnp.broadcast_to(tag_row, (TOK, TOK)), 0.0), axis=1, keepdims=True)
-    tag_block = jnp.broadcast_to(tag_col, (TOK, TAG)).astype(BF16)
-    for h in range(2):
-        hid[d, h, :, pl.ds(half, TAG)] = tag_block
+    seat_t = xh * 4 + y
+    tags_ref[core, seat_t] = jnp.broadcast_to(tag_col, (TOK, TAG)).astype(BF16)
+    pl.semaphore_wait(barrier, 2 * (PAIR - 1))
+
+    up, down, far = (y + 1) % 4, (y + 3) % 4, (y + 2) % 4
+    other = 1 - xh
+    cross_x = other * 2 + 1 - xl
+    colour = (z + 2 * xl) % 4
+    to_sib = place(x, y, 1 - core, z)
+    to_twin = place(xh * 2 + 1 - xl, y, core, z)
+    to_above = place(x, y, core, (z + 1) % DEPTH)
+    to_below = place(x, y, core, (z + DEPTH - 1) % DEPTH)
+
+    def spot(n, rq, of_core=core):
+        row = group(xh if n < 4 else other, (y, up, down, far)[n % 4], of_core)
+        return hid.at[row, (colour + rq) % 4]
+
+    fetches = (
+        (place(cross_x, y, core, z), 4, 2, (0, 1, 3)),
+        (place(x, down, core, z), 1, 0, (0, 2, 1)),
+        (place(x, up, core, z), 2, 0, (0, 2, 3)),
+        (place(x, far, core, z), 3, 0, (0,)),
+        (place(cross_x, down, core, z), 5, 2, (0,)),
+        (place(cross_x, up, core, z), 6, 2, (0,)),
+        (place(cross_x, far, core, z), 7, 2, (0,)),
+    )
+    count = 0
+    for level in range(3):
+        for device, n, shift, quarters in fetches:
+            if level < len(quarters):
+                rq = quarters[level]
+                q = (colour + shift + rq) % 4
+                src = hidden_ref.at[:, pl.ds(pl.multiple_of(q * quad, quad), quad)]
+                launch(remote(src, hid.at[d, q], g_send.at[count], g_recv.at[n * 4 + rq], device))
+                count += 1
+    own_tags = tags_ref.at[core, seat_t]
+    for device, n, _, _ in fetches:
+        launch(remote(own_tags, own_tags, t_send.at[n], t_recv.at[n], device))
     for copy in h_copies:
         copy.wait()
-    pl.semaphore_wait(barrier, 2 * (PAIR - 1))
-
-    up, down = (y + 1) % 4, (y + 3) % 4
-    far = (y + 2) % 4
-    to_up, to_down = place(x, up, core, z), place(x, down, core, z)
-    other = 1 - xh
-    to_cross = place(other * 2 + 1 - xl, y, core, z)
-    to_twin = place(xh * 2 + 1 - xl, y, core, z)
-    to_sib = place(x, y, 1 - core, z)
-    sent = []
-
-    def gsend(k, chunk, device):
-        copy = remote(chunk, chunk, g_send.at[k], g_recv.at[k], device)
-        copy.start()
-        sent.append(copy)
-
-    def gwait(k, chunk):
-        remote(chunk, chunk, g_send.at[k], g_recv.at[k], to_sib).wait_recv()
-
-    own = hid.at[d]
-    c_down, c_up, c_far = (hid.at[group(xh, yy, core)] for yy in (down, up, far))
-    cross_y = (y, down, up, far)
-
-    gsend(0, own, to_up)
-    gsend(1, own, to_down)
-    gsend(2, hid.at[d, 1 - xl], to_cross)
-    gsend(3, own, to_sib)
-
-    def crossed(i, k):
-        chunk = hid.at[group(other, cross_y[i], core), xl]
-        gwait(k, chunk)
-        gsend(12 + i, chunk, to_twin)
-        gsend(16 + i, chunk, to_sib)
-
-    crossed(0, 2)
-    gwait(0, c_down)
-    gsend(4, hid.at[group(xh, down, core), 0], to_up)
-    gsend(5, hid.at[group(xh, down, core), 1 - xl], to_cross)
-    gsend(6, c_down, to_sib)
-    gwait(1, c_up)
-    gsend(7, hid.at[group(xh, up, core), 1], to_down)
-    gsend(8, hid.at[group(xh, up, core), 1 - xl], to_cross)
-    gsend(9, c_up, to_sib)
-    gwait(4, hid.at[group(xh, far, core), 0])
-    gwait(7, hid.at[group(xh, far, core), 1])
-    gsend(10, hid.at[group(xh, far, core), 1 - xl], to_cross)
-    gsend(11, c_far, to_sib)
-    crossed(1, 5)
-    crossed(2, 8)
-    crossed(3, 10)
-    for i in range(4):
-        chunk = hid.at[group(other, cross_y[i], core), 1 - xl]
-        gwait(12 + i, chunk)
-        gsend(20 + i, chunk, to_sib)
-
+
+    def hand_over(n, rq):
+        chunk = spot(n, rq)
+        launch(remote(chunk, chunk, h_send.at[n * 4 + rq], h_recv.at[n * 4 + rq], to_sib))
+
+    def arrived(n, rq):
+        chunk = spot(n, rq)
+        remote(chunk, chunk, g_send.at[0], g_recv.at[n * 4 + rq], to_sib).wait_recv()
+
+    for rq in range(4):
+        hand_over(0, rq)
     for copy in w_copies:
         copy.wait()
     w_swap = remote(w.at[1 - core], wsib, e_send.at[0], e_recv.at[0], to_sib)
-    w_swap.start()
-
-    gwait(3, hid.at[group(xh, y, 1 - core)])
-    gwait(6, hid.at[group(xh, down, 1 - core)])
-    gwait(9, hid.at[group(xh, up, 1 - core)])
-    gwait(11, hid.at[group(xh, far, 1 - core)])
-    for i in range(4):
-        gwait(16 + i, hid.at[group(other, cross_y[i], 1 - core), xl])
-        gwait(20 + i, hid.at[group(other, cross_y[i], 1 - core), 1 - xl])
+    launch(w_swap)
+
+    for n in (4, 1, 2, 3, 5, 6, 7):
+        arrived(n, 0)
+        chunk = spot(n, 0)
+        for device, rq, skipped in ((to_twin, 2, (1, 2)), (to_above, 3, (2, 4)), (to_below, 1, (1, 4))):
+            if n not in skipped:
+                launch(remote(chunk, chunk, g_send.at[count], g_recv.at[n * 4 + rq], device))
+                count += 1
+        hand_over(n, 0)
+    for n in range(1, 8):
+        there = tags_ref.at[core, (xh if n < 4 else other) * 4 + (y, up, down, far)[n % 4]]
+        remote(there, there, t_send.at[n], t_recv.at[n], to_sib).wait_recv()
+    launch(remote(tags_ref.at[core], tags_ref.at[core], t_send.at[0], t_recv.at[0], to_sib))
+    for n in (4, 1, 2, 3, 5, 6, 7):
+        for rq in (2, 3, 1):
+            arrived(n, rq)
+            hand_over(n, rq)
+
+    remote(tags_ref.at[1 - core], tags_ref.at[1 - core], t_send.at[0], t_recv.at[0], to_sib).wait_recv()
+    for n in range(8):
+        for rq in range(4):
+            chunk = spot(n, rq, 1 - core)
+            remote(chunk, chunk, h_send.at[0], h_recv.at[n * 4 + rq], to_sib).wait_recv()
 
     tokens = GROUPS * TOK
-    deep = min(512, half)
+    deep = min(512, quad)
     per_half = half // deep
-
-    logit[...] = jnp.broadcast_to(bias_ref[...], (tokens, voc))
+    per_quad = quad // deep
+
+    logit[...] = jnp.broadcast_to(rows_ref[0:1, :], (tokens, voc))
 
     def logit_step(i, carry):
-        h = i // per_half
-        start = pl.multiple_of((i % per_half) * deep, deep)
-        a = hid[:, h, :, pl.ds(start, deep)].reshape(tokens, deep)
-        logit[...] += dot(a, w[h, pl.ds(start, deep), :])
+        start = pl.multiple_of((i % per_quad) * deep, deep)
+        a = hid[:, i // per_quad, :, pl.ds(start, deep)].reshape(tokens, deep)
+        rows = pl.ds(pl.multiple_of((i % per_half) * deep, deep), deep)
+        logit[...] += dot(a, w[i // per_half, rows, :])
         return carry
 
     lax.fori_loop(0, 2 * per_half, logit_step, 0)
 
-    tags = hid[:, 0, :, pl.ds(half, TAG)].reshape(tokens, TAG).astype(F32)
+    by_group = [tags_ref[c, gxh * 4 + gy] for gxh in range(2) for gy in range(4) for c in range(2)]
+    tags = jnp.concatenate(by_group, axis=0).astype(F32)
     lane = iota((tokens, TAG), 1)
     index = lane % 32
     wanted_group = index // 2
@@ -195,7 +207,8 @@
         & (lane < 64)
     )
     member_t = jnp.where(belongs, 1.0, 0.0)
-    mt[...] = member_t.astype(BF16)
+    for i in range(3):
+        mt[:, pl.ds(i * TAG, TAG)] = member_t.astype(BF16)
     member = jnp.transpose(member_t)
     inv_count = 1.0 / jnp.maximum(jnp.sum(member, axis=1, keepdims=True), 1.0)
     member = member.astype(BF16)
@@ -233,7 +246,7 @@
         remote(ara.at[slot], ara.at[slot], a_send.at[k], a_recv.at[k], column_mate(k)) for k in range(1, PAIR)
     ]
     for copy in a_copies:
-        copy.start()
+        launch(copy)
 
     def factor_step(i, carry):
         rows = pl.ds(pl.multiple_of(i * TOK, TOK), TOK)
@@ -258,7 +271,7 @@
         remote(arb.at[slot_b], arb.at[slot_b], b_send.at[k], b_recv.at[k], plane_mate(k)) for k in range(1, PAIR)
     ]
     for copy in b_copies:
-        copy.start()
+        launch(copy)
     for copy in b_copies:
         copy.wait_recv()
     total = arb[0]
@@ -280,7 +293,7 @@
     exp_scores = jnp.where(in_passages, jnp.exp(scores), 0.0)
     totals = jnp.sum(exp_scores, axis=0, keepdims=True)
     totals = jnp.where(in_passages[0:1], totals, 1.0)
-    labels = labels_ref[...].astype(F32)
+    labels = rows_ref[1:2, 0:32]
     label_col = jnp.sum(jnp.where(eye, jnp.broadcast_to(labels, (32, 32)), 0.0), axis=1, keepdims=True)
     row_id = iota((32, TAG), 0)
     label_row = jnp.sum(
@@ -301,50 +314,68 @@
     pooled_grad = (dot(grad_sym, unit, precision=precise) - unit * radial) * inv_norm
     sum_grad = pooled_grad * inv_count / (4.0 * (1.0 + pooled_sum))
 
-    s1, s2, s3 = split3(sum_grad)
-    new, old = iota((64, 64), 0), iota((64, 64), 1)
-    source = ((new // 16) % 2) * 32 + ((new // 2) % 8) * 4 + (new // 32) * 2 + new % 2
+    thirds = jnp.concatenate(split3(sum_grad), axis=0)
+    new, old = iota((128, 128), 0), iota((128, 128), 1)
+    source = (new // 64) * 64 + ((new // 16) % 2) * 32 + ((new // 2) % 8) * 4 + ((new // 32) % 2) * 2 + new % 2
     shuffle = jnp.where(source == old, 1.0, 0.0).astype(BF16)
-
-    def grad_step(i, carry):
-        rows = pl.ds(pl.multiple_of(i * 64, 64), 64)
-        m = mt[rows, :]
-        g = (dot(m, s1) + dot(m, s2) + dot(m, s3)) * fac[rows, :]
-        g = g.astype(BF16)
+    lg_swaps = []
+    for i in range(4):
+        rows = pl.ds(i * 128, 128)
+        g = (dot(mt[rows, :], thirds) * fac[rows, :]).astype(BF16)
         lg[rows, :] = g
         p = dot(shuffle, g).astype(BF16)
-        lgp[(i // 4) * 2, i % 4] = p[:32]
-        lgp[(i // 4) * 2 + 1, i % 4] = p[32:]
-        return carry
-
-    lax.fori_loop(0, 8, grad_step, 0)
-    lg_swap = remote(lgp, lgs, e_send.at[1], e_recv.at[1], to_sib)
-    lg_swap.start()
-    w_swap.wait_recv()
-    lg_swap.wait_recv()
+        box = (pl.ds((i // 2) * 2, 2), pl.ds((i % 2) * 2, 2))
+        for b in range(4):
+            lgp[(i // 2) * 2 + b % 2, (i % 2) * 2 + b // 2] = p[b * 32 : b * 32 + 32]
+        swap = remote(lgp.at[box], lgs.at[box], e_send.at[1 + i], e_recv.at[1 + i], to_sib)
+        launch(swap)
+        lg_swaps.append(swap)
 
     block = min(512, half)
 
+    def rows_of(ref, o):
+        picked = []
+        for i in range(4):
+            px = (1 - core) * ((x + o) % 4) + core * i
+            py = core * ((y + o) % 4) + (1 - core) * i
+            picked.append(ref[px, py])
+        return jnp.concatenate(picked, axis=0)
+
+    def columns(n):
+        return pl.ds(pl.multiple_of(n * block, block), block)
+
     def partial(o):
-        def rows_of(ref):
-            picked = []
-            for i in range(4):
-                px = (1 - core) * ((x + o) % 4) + core * i
-                py = core * ((y + o) % 4) + (1 - core) * i
-                picked.append(ref[px, py])
-            return jnp.concatenate(picked, axis=0)
-
-        mine, theirs = rows_of(lgp), rows_of(lgs)
+        mine, theirs = rows_of(lgp, o), rows_of(lgs, o)
 
         def step(n, carry):
-            start = pl.multiple_of(n * block, block)
-            cols = pl.ds(start, block)
+            cols = columns(n)
             value = dot(mine, w[core, cols, :], ((1,), (1,))) + dot(theirs, wsib[cols, :], ((1,), (1,)))
             part[o, :, :, cols] = value.astype(BF16).reshape(4, 32, block)
             return carry
 
         lax.fori_loop(0, half // block, step, 0)
 
+    mine = rows_of(lgp, 2)
+
+    def first_step(n, carry):
+        cols = columns(n)
+        pre[:, cols] = dot(mine, w[core, cols, :], ((1,), (1,)))
+        return carry
+
+    lax.fori_loop(0, half // block, first_step, 0)
+    w_swap.wait_recv()
+    for swap in lg_swaps:
+        swap.wait_recv()
+    theirs = rows_of(lgs, 2)
+
+    def second_step(n, carry):
+        cols = columns(n)
+        value = pre[:, cols] + dot(theirs, wsib[cols, :], ((1,), (1,)))
+        part[2, :, :, cols] = value.astype(BF16).reshape(4, 32, block)
+        return carry
+
+    lax.fori_loop(0, half // block, second_step, 0)
+
     quarter = half // 2
     left, right = pl.ds(0, quarter), pl.ds(quarter, quarter)
 
@@ -355,41 +386,33 @@
         return place((x + core * o) % 4, (y + (1 - core) * o) % 4, core, z)
 
     plus, minus = ring(1), ring(3)
-    partial(2)
     far_l = remote(part.at[2, :, :, left], farl, r_send.at[0], r_recv.at[0], plus)
     far_r = remote(part.at[2, :, :, right], farr, r_send.at[1], r_recv.at[1], minus)
-    far_l.start()
-    far_r.start()
+    launch(far_l)
+    launch(far_r)
     partial(1)
     plain_r = remote(part.at[1, :, :, right], fromm.at[1], r_send.at[2], r_recv.at[2], plus)
-    plain_r.start()
+    launch(plain_r)
     partial(3)
     plain_l = remote(part.at[3, :, :, left], fromp.at[0], r_send.at[3], r_recv.at[3], minus)
-    plain_l.start()
+    launch(plain_l)
     partial(0)
     far_l.wait_recv()
     part[1, :, :, left] = (part[1, :, :, left].astype(F32) + farl[...].astype(F32)).astype(BF16)
     sum_l = remote(part.at[1, :, :, left], fromm.at[0], r_send.at[4], r_recv.at[4], plus)
-    sum_l.start()
+    launch(sum_l)
     far_r.wait_recv()
     part[3, :, :, right] = (part[3, :, :, right].astype(F32) + farr[...].astype(F32)).astype(BF16)
     sum_r = remote(part.at[3, :, :, right], fromp.at[1], r_send.at[5], r_recv.at[5], minus)
-    sum_r.start()
+    launch(sum_r)
 
     def weight_step(i, carry):
-        h = i // per_half
-        start = pl.multiple_of((i % per_half) * deep, deep)
-        a = hid[:, h, :, pl.ds(start, deep)].reshape(tokens, deep)
-        wg[h, pl.ds(start, deep), :] = dot(a, lg[...], ((0,), (0,))).astype(BF16)
+        start = pl.multiple_of((i % per_quad) * deep, deep)
+        a = hid[:, i // per_quad, :, pl.ds(start, deep)].reshape(tokens, deep)
+        wgrad_ref[pl.ds(pl.multiple_of(i * deep, deep), deep), :] = dot(a, lg[...], ((0,), (0,))).astype(BF16)
         return carry
 
     lax.fori_loop(0, 2 * per_half, weight_step, 0)
-    wg_copies = [
-        pltpu.make_async_copy(wg.at[h], wgrad_ref.at[pl.ds(h * half, half), :], loc_sem.at[4 + h]) for h in range(2)
-    ]
-    for copy in wg_copies:
-        copy.start()
-
     for copy in (plain_r, plain_l, sum_l, sum_r):
         copy.wait_recv()
     for h, cols in ((0, left), (1, right)):
@@ -402,7 +425,7 @@
         for o in range(1, 4)
     ]
     for copy in two_copies:
-        copy.start()
+        launch(copy)
     for copy in two_copies:
         copy.wait_recv()
     rows = acc[seat].astype(F32)
@@ -420,7 +443,7 @@
     for k in range(1, PAIR):
         target = ((core + k // DEPTH) % 2) * DEPTH + (z + k % DEPTH) % DEPTH
         copy = remote(zsend.at[target], zrecv.at[slot], z_send.at[k], z_recv.at[k], column_mate(k))
-        copy.start()
+        launch(copy)
         z_copies.append(copy)
     zrecv[slot] = zsend[slot]
     for copy in z_copies:
@@ -433,20 +456,25 @@
             for b in range(8):
                 hgrad_ref[r : r + 1, pl.ds(c * half + b * slab, slab)] = value[r * 8 + b : r * 8 + b + 1]
 
-    for copy in sent + [w_swap, lg_swap] + a_copies + b_copies:
+    for copy in sent:
         copy.wait_send()
-    for copy in [far_l, far_r, plain_r, plain_l, sum_l, sum_r] + two_copies + z_copies:
-        copy.wait_send()
-    for copy in wg_copies:
-        copy.wait()
 
 
 def body(hidden, head_weight, vocab_bias, seq_ids, token_mask, labels):
     width, voc = head_weight.shape
     half = width // 2
     tokens = GROUPS * TOK
+    tag = jnp.where(token_mask > 0, seq_ids, SEQ_GROUP).astype(F32)
+    rows = jnp.concatenate(
+        [
+            vocab_bias[None, :],
+            jnp.pad(labels.astype(F32)[None, :], ((0, 0), (0, voc - labels.shape[0]))),
+            jnp.pad(tag, ((0, 5), (0, voc - TOK))),
+        ],
+        axis=0,
+    )
     vmem = pl.BlockSpec(memory_space=pltpu.VMEM)
-    hbm = pl.BlockSpec(memory_space=pl.ANY)
+    hbm = pl.BlockSpec(memory_space=pltpu.HBM)
     dma = pltpu.SemaphoreType.DMA
     loss, weight_grad, hidden_grad = pl.pallas_call(
         fused,
@@ -455,21 +483,23 @@
             jax.ShapeDtypeStruct((width, voc), BF16),
             jax.ShapeDtypeStruct((2, width), F32),
         ),
-        in_specs=[hbm, hbm, vmem, vmem, vmem, vmem],
-        out_specs=(vmem, hbm, vmem),
+        in_specs=[hbm, hbm, vmem],
+        out_specs=(vmem, vmem, vmem),
         scratch_shapes=[
-            pltpu.VMEM((GROUPS, 2, TOK, half + TAG), BF16),
+            pltpu.VMEM((GROUPS, 4, TOK, width // 4), BF16),
+            pltpu.VMEM((2, GROUPS // 2, TOK, TAG), BF16),
             pltpu.VMEM((2, half, voc), BF16),
             pltpu.VMEM((half, voc), BF16),
             pltpu.VMEM((tokens, voc), F32),
             pltpu.VMEM((tokens, voc), F32),
             pltpu.VMEM((tokens, voc), F32),
-            pltpu.VMEM((tokens, TAG), BF16),
+            pltpu.VMEM((tokens, 3 * TAG), BF16),
             pltpu.VMEM((tokens, voc), BF16),
             pltpu.VMEM((4, 4, TOK, voc), BF16),
             pltpu.VMEM((4, 4, TOK, voc), BF16),
             pltpu.VMEM((PAIR, 16, TAG), F32),
             pltpu.VMEM((PAIR, 16, TAG), F32),
+            pltpu.VMEM((4 * TOK, half), F32),
             pltpu.VMEM((4, 4, TOK, half), BF16),
             pltpu.VMEM((4, TOK, half // 2), BF16),
             pltpu.VMEM((4, TOK, half // 2), BF16),
@@ -479,12 +509,15 @@
             pltpu.VMEM((3, TOK, half), BF16),
             pltpu.VMEM((PAIR, 16, half // 8), BF16),
             pltpu.VMEM((PAIR, 16, half // 8), BF16),
-            pltpu.VMEM((2, half, voc), BF16),
             dma((6,)),
             dma((GATHER_COPIES,)),
-            dma((GATHER_COPIES,)),
-            dma((2,)),
-            dma((2,)),
+            dma((32,)),
+            dma((32,)),
+            dma((32,)),
+            dma((8,)),
+            dma((8,)),
+            dma((5,)),
+            dma((5,)),
             dma((PAIR,)),
             dma((PAIR,)),
             dma((PAIR,)),
@@ -500,14 +533,7 @@
             collective_id=0, has_side_effects=True, vmem_limit_bytes=48 * 1024 * 1024
         ),
         name="splade_head",
-    )(
-        hidden,
-        head_weight,
-        vocab_bias.reshape(1, voc),
-        seq_ids,
-        token_mask,
-        labels.reshape(1, labels.shape[0]),
-    )
+    )(hidden, head_weight, rows)
     return loss.reshape(()), weight_grad, hidden_grad
 
 

time: 94.1 us -> 82.8 us (0.88)
  Pallas kernels: 85.7 us -> 75 us
  local copies, waits for them, and re-layouts: 5.88 us -> 3.91 us
  other arithmetic: 0 us -> 1.35 us
    pallas_call x1, Pallas kernels: 85.7 us -> 75 us  [body(): pl.pallas_call(fused, out_shape=(jax.ShapeDtypeStruct((1, 1), F32), jax.S...]
    unnamed x10 -> x4, local copies, waits for them, and re-layouts: 5.19 us -> 3.22 us
where the time goes in v2:
time: 82.8 us; the launch traced here: 82.7 us
  Pallas kernels  75 us (91%)
  local copies, waits for them, and re-layouts  3.91 us (5%)
  between operations  2.41 us (3%)
  other arithmetic  1.35 us (2%)
    pallas_call x1, Pallas kernels, body(): pl.pallas_call(fused, out_shape=(jax.ShapeDtypeStruct((1, 1), F32), jax.S...  75 us
    unnamed x4, local copies, waits for them, and re-layouts  3.22 us

profile of v2, /device:TPU:1, one launch (start us, length us, event | category | flops | bytes accessed | tf_op | source)
XLA Modules:
  0.0 82.7 jit_solution(8607188418061758716)
XLA Ops:
  0.6 0.7 fusion.1
  1.3 0.7 convert_bitcast_fusion
  2.0 0.7 broadcast_in_dim.10
  2.7 0.0 copy-start
  2.7 0.9 %copy-done = bf16[32,4096]{1,0:T(8,128)(2,1)S(1)} copy-done((bf16[32,4096]{1,0:T(8,128)(2,1)S(1)}, bf16[32,4096]{1,0:T(8,128)(2,1)}, u32[]{:S(2)}) %copy-start) | copy-done | bytes 262168
  3.6 75.0 %splade_head.1 = (f32[1,1]{1,0:T(1,128)}, bf16[4096,384]{1,0:T(8,128)(2,1)S(1)}, f32[2,4096]{1,0:T(2,128)S(1)}) custom-call(bf16[32,4096]{1,0:T(8,128)(2,1)S(1)} %copy-done, bf16[4096,384]{1,0:T(8,128)(2,1)} %weight_ref.1, f32[8,384]{1,0:T(8,128)S(1)} %select_maximum_fusion.rows_ref), custom_call_target="tpu_custom_call" | custom-call | tf_op jit(solution)/shard_map/splade_head/pallas_call | solution.py:479
  79.3 1.7 %copy.13 = bf16[4096,384]{1,0:T(8,128)(2,1)} copy(bf16[4096,384]{1,0:T(8,128)(2,1)S(1)} %get-tuple-element.13) | data formatting | bytes 6291456
  80.9 0.6 copy.14
  (1 shorter events, 0.0 us)
Async XLA Ops:
  2.7 1.0 %copy-start = (bf16[32,4096]{1,0:T(8,128)(2,1)S(1)}, bf16[32,4096]{1,0:T(8,128)(2,1)}, u32[]{:S(2)}) copy-start(bf16[32,4096]{1,0:T(8,128)(2,1)} %hidden_ref.1) | copy-start | bytes 786436

commit v3 on v2

v3 whole, which is shorter than its diff:
```python
import functools

import jax
import jax.numpy as jnp
from jax import lax
from jax.experimental import pallas as pl
from jax.experimental.pallas import tpu as pltpu
from jax.sharding import PartitionSpec as P

MESH = pl.DeviceIdType.MESH
F32, BF16 = jnp.float32, jnp.bfloat16

SEQ_GROUP = 4
GROUPS = 16
TOK = 32
SIDE = 4
DEPTH = 8
TAG = 128

score_scale = 20.0
loss_scale = 65536.0
norm_eps = 1e-06
precise = lax.Precision.HIGHEST

GATHER_COPIES = 28
PAIR = 16
CHUNKS = 8


def iota(shape, dim):
    return lax.broadcasted_iota(jnp.int32, shape, dim)


def split3(x):
    first = x.astype(BF16)
    rest = x - first.astype(F32)
    second = rest.astype(BF16)
    third = (rest - second.astype(F32)).astype(BF16)
    return first, second, third


def dot(a, b, dims=((1,), (0,)), precision=None):
    return lax.dot_general(a, b, (dims, ((), ())), precision=precision, preferred_element_type=F32)


def fused(
    hidden_ref, weight_ref, bias_hbm, seq_hbm, mask_hbm, labels_hbm,
    loss_ref, wgrad_hbm, hgrad_ref,
    bias_ref, seq_ref, mask_ref, labels_ref, wgrad_ref,
    hid, tags_ref, w, wsib, logit, fac, excess, mt, lg, lgp, lgs,
    ara, arb, pre, part, fars_in, fromm, fromp, acc, rtwo, zsend, zrecv,
    loc_sem, g_send, g_recv, h_send, h_recv, t_send, t_recv, e_send, e_recv, a_send, a_recv, b_send, b_recv,
    r_send, r_recv, s_send, s_recv, z_send, z_recv,
):
    width = hidden_ref.shape[1]
    half = width // 2
    voc = weight_ref.shape[1]
    d, v = lax.axis_index("dp"), lax.axis_index("vocab")
    core, y, xh = d % 2, (d // 2) % 4, d // 8
    xl, z = v % 2, v // 2
    x = xh * 2 + xl

    def place(px, py, pc, pz):
        return ((px // 2) * 8 + py * 2 + pc, pz * 2 + px % 2)

    def column_mate(k):
        return place(x, y, (core + k // DEPTH) % 2, (z + k % DEPTH) % DEPTH)

    def plane_mate(k):
        return place((x + k // SIDE) % SIDE, (y + k % SIDE) % SIDE, core, z)

    def remote(src, dst, send, recv, device):
        return pltpu.make_async_remote_copy(
            src_ref=src, dst_ref=dst, send_sem=send, recv_sem=recv, device_id=device, device_id_type=MESH
        )

    sent = []

    def launch(copy):
        copy.start()
        sent.append(copy)

    w_copies = [
        pltpu.make_async_copy(weight_ref.at[pl.ds(h * half, half), :], w.at[h], loc_sem.at[h]) for h in range(2)
    ]
    quad = width // 4
    seat_t = xh * 4 + y
    h_copies = [
        pltpu.make_async_copy(hidden_ref.at[:, pl.ds(q * quad, quad)], hid.at[core, seat_t, q], loc_sem.at[2 + q])
        for q in range(4)
    ]
    small_copies = [
        pltpu.make_async_copy(src, dst, loc_sem.at[6 + i])
        for i, (src, dst) in enumerate(
            ((seq_hbm, seq_ref), (mask_hbm, mask_ref), (bias_hbm, bias_ref), (labels_hbm, labels_ref))
        )
    ]
    for copy in small_copies[:2] + h_copies + w_copies + small_copies[2:]:
        copy.start()

    barrier = pltpu.get_barrier_semaphore()
    for k in range(1, PAIR):
        pl.semaphore_signal(barrier, inc=1, device_id=column_mate(k), device_id_type=MESH)
        pl.semaphore_signal(barrier, inc=1, device_id=plane_mate(k), device_id_type=MESH)

    eye = iota((TOK, TOK), 0) == iota((TOK, TOK), 1)
    for copy in small_copies[:2]:
        copy.wait()
    tag_row = jnp.where(mask_ref[...] > 0, seq_ref[...], SEQ_GROUP).astype(F32)
    tag_col = jnp.sum(jnp.where(eye, jnp.broadcast_to(tag_row, (TOK, TOK)), 0.0), axis=1, keepdims=True)
    tags_ref[core, seat_t] = jnp.broadcast_to(tag_col, (TOK, TAG)).astype(BF16)
    pl.semaphore_wait(barrier, 2 * (PAIR - 1))

    up, down, far = (y + 1) % 4, (y + 3) % 4, (y + 2) % 4
    other = 1 - xh
    cross_x = other * 2 + 1 - xl
    colour = (z + 2 * xl) % 4
    to_sib = place(x, y, 1 - core, z)
    to_twin = place(xh * 2 + 1 - xl, y, core, z)
    to_above = place(x, y, core, (z + 1) % DEPTH)
    to_below = place(x, y, core, (z + DEPTH - 1) % DEPTH)

    def spot(n, rq, of_core=core):
        row = (xh if n < 4 else other) * 4 + (y, up, down, far)[n % 4]
        return hid.at[of_core, row, (colour + rq) % 4]

    fetches = (
        (place(cross_x, y, core, z), 4, 2, (0, 1, 3)),
        (place(x, down, core, z), 1, 0, (0, 2, 1)),
        (place(x, up, core, z), 2, 0, (0, 2, 3)),
        (place(x, far, core, z), 3, 0, (0,)),
        (place(cross_x, down, core, z), 5, 2, (0,)),
        (place(cross_x, up, core, z), 6, 2, (0,)),
        (place(cross_x, far, core, z), 7, 2, (0,)),
    )
    free_sends = iter(range(GATHER_COPIES))

    def post(chunks, levels):
        for level in levels:
            for device, n, shift, quarters in fetches:
                if n in chunks and level < len(quarters):
                    rq = quarters[level]
                    q = (colour + shift + rq) % 4
                    src = hid.at[core, seat_t, q]
                    launch(remote(src, src, g_send.at[next(free_sends)], g_recv.at[n * 4 + rq], device))

    for copy in h_copies:
        copy.wait()
    post((1, 2, 3, 4, 5, 6, 7), (0,))
    own_tags = tags_ref.at[core, seat_t]
    for device, n, _, _ in fetches:
        launch(remote(own_tags, own_tags, t_send.at[n], t_recv.at[n], device))

    def hand_over(n, rq):
        chunk = spot(n, rq)
        launch(remote(chunk, chunk, h_send.at[n * 4 + rq], h_recv.at[n * 4 + rq], to_sib))

    def arrived(n, rq):
        chunk = spot(n, rq)
        remote(chunk, chunk, g_send.at[0], g_recv.at[n * 4 + rq], to_sib).wait_recv()

    for rq in range(4):
        hand_over(0, rq)
    for copy in w_copies + small_copies[2:]:
        copy.wait()
    w_swap = remote(w.at[1 - core], wsib, e_send.at[0], e_recv.at[0], to_sib)
    launch(w_swap)

    for n in (4, 1, 2, 3, 5, 6, 7):
        arrived(n, 0)
        chunk = spot(n, 0)
        for device, rq, skipped in ((to_twin, 2, (1, 2)), (to_above, 3, (2, 4)), (to_below, 1, (1, 4))):
            if n not in skipped:
                launch(remote(chunk, chunk, g_send.at[next(free_sends)], g_recv.at[n * 4 + rq], device))
        if n == 4:
            post((1, 2, 4), (1,))
        if n == 3:
            post((1, 2, 4), (2,))
        hand_over(n, 0)
    for n in range(1, 8):
        there = tags_ref.at[core, (xh if n < 4 else other) * 4 + (y, up, down, far)[n % 4]]
        remote(there, there, t_send.at[n], t_recv.at[n], to_sib).wait_recv()
    launch(remote(tags_ref.at[core], tags_ref.at[core], t_send.at[0], t_recv.at[0], to_sib))
    for n in (4, 1, 2, 3, 5, 6, 7):
        for rq in (2, 3, 1):
            arrived(n, rq)
            hand_over(n, rq)

    tokens = GROUPS * TOK
    deep = min(512, quad)
    per_half = half // deep
    per_quad = quad // deep

    share = tokens // 2

    def logits_of(c):
        rows = pl.ds(pl.multiple_of(c * share, share), share)
        for b in range(voc // TAG):
            logit[rows, pl.ds(b * TAG, TAG)] = jnp.broadcast_to(bias_ref[b : b + 1, :], (share, TAG))

        def step(q, carry):
            a = hid[c, :, q].reshape(share, quad)
            logit[rows, :] += dot(a, w[q // 2, pl.ds(pl.multiple_of((q % 2) * quad, quad), quad), :])
            return carry

        lax.fori_loop(0, 4, step, 0)

    logits_of(core)

    remote(tags_ref.at[1 - core], tags_ref.at[1 - core], t_send.at[0], t_recv.at[0], to_sib).wait_recv()
    for n in range(8):
        for rq in range(4):
            chunk = spot(n, rq, 1 - core)
            remote(chunk, chunk, h_send.at[0], h_recv.at[n * 4 + rq], to_sib).wait_recv()

    logits_of(1 - core)

    tags = tags_ref[...].reshape(tokens, TAG).astype(F32)
    row = iota((tokens, TAG), 0)
    lane = iota((tokens, TAG), 1)
    index = lane % 32
    wanted_group = index // 2
    wanted_tag = index % 2 + 2 * (lane // 32)
    belongs = (
        (2 * ((row % share) // TOK) + row // share == wanted_group)
        & (tags == wanted_tag.astype(F32))
        & (tags < SEQ_GROUP)
        & (lane < 64)
    )
    member_t = jnp.where(belongs, 1.0, 0.0)
    for i in range(3):
        mt[:, pl.ds(i * TAG, TAG)] = member_t.astype(BF16)
    member = jnp.transpose(member_t)
    inv_count = 1.0 / jnp.maximum(jnp.sum(member, axis=1, keepdims=True), 1.0)
    member = member.astype(BF16)

    def excess_step(i, carry):
        rows = pl.ds(pl.multiple_of(i * TOK, TOK), TOK)
        l = logit[rows, :]
        soft = jnp.maximum(l, 0.0) + jnp.log1p(jnp.exp(-jnp.abs(l)))
        u = 1.0 + jnp.log1p(soft)
        u2 = u * u
        excess[rows, :] = u2 * u2 - 1.0
        return carry

    lax.fori_loop(0, GROUPS, excess_step, 0)
    e1, e2, e3 = split3(excess[...])
    pooled_sum = (dot(member, e1) + dot(member, e2) + dot(member, e3)) * inv_count
    pooled = jnp.log1p(pooled_sum) * 0.25

    wide = iota((32, TAG), 1)
    in_passages = (wide >= 32) & (wide < 64)
    inner = dot(pooled[:32], pooled, ((1,), (1,)), precise)
    inner = jnp.where(in_passages, inner, 0.0)
    packed = inner[0:8]
    packed = pltpu.roll(packed, 96, 1)
    for b in range(1, 4):
        shift = 32 * (b - 1)
        piece = inner[8 * b : 8 * b + 8]
        packed = packed + (pltpu.roll(piece, shift, 1) if shift else piece)
    squares = dot(jnp.ones((8, voc), F32), pooled * pooled, ((1,), (1,)), precise)

    slot = core * DEPTH + z
    ara[slot, 0:8, :] = packed
    ara[slot, 8:9, :] = squares[0:1]
    message = pl.ds(0, 9)
    a_copies = [
        remote(ara.at[slot, message], ara.at[slot, message], a_send.at[k], a_recv.at[k], column_mate(k))
        for k in range(1, PAIR)
    ]
    for copy in a_copies:
        launch(copy)

    def factor_step(i, carry):
        rows = pl.ds(pl.multiple_of(i * TOK, TOK), TOK)
        l = logit[rows, :]
        e = jnp.exp(-jnp.abs(l))
        soft = jnp.maximum(l, 0.0) + jnp.log1p(e)
        u = 1.0 + jnp.log1p(soft)
        top = jnp.where(l >= 0.0, 1.0, e)
        fac[rows, :] = 4.0 * (u * u * u) * top / ((1.0 + e) * (1.0 + soft))
        return carry

    lax.fori_loop(0, GROUPS, factor_step, 0)

    for copy in a_copies:
        copy.wait_recv()
    column_sum = ara[0, message]
    for k in range(1, PAIR):
        column_sum = column_sum + ara[k, message]
    slot_b = x * SIDE + y
    arb[slot_b, message] = column_sum
    b_copies = [
        remote(arb.at[slot_b, message], arb.at[slot_b, message], b_send.at[k], b_recv.at[k], plane_mate(k))
        for k in range(1, PAIR)
    ]
    for copy in b_copies:
        launch(copy)
    for copy in b_copies:
        copy.wait_recv()
    total = arb[0, message]
    for k in range(1, PAIR):
        total = total + arb[k, message]

    pieces = []
    for b in range(4):
        shift = (32 - 32 * b) % 128
        pieces.append(pltpu.roll(total[0:8], shift, 1) if shift else total[0:8])
    inner = jnp.where(in_passages, jnp.concatenate(pieces, axis=0), 0.0)
    square_row = total[8:9]
    eye_wide = iota((TAG, TAG), 0) == iota((TAG, TAG), 1)
    square_col = jnp.sum(jnp.where(eye_wide, jnp.broadcast_to(square_row, (TAG, TAG)), 0.0), axis=1, keepdims=True)
    norm_row = jnp.sqrt(square_row + norm_eps)
    norm_col = jnp.sqrt(square_col + norm_eps)
    cosine = inner / (norm_col[:32] * norm_row)
    scores = score_scale * cosine
    exp_scores = jnp.where(in_passages, jnp.exp(scores), 0.0)
    totals = jnp.sum(exp_scores, axis=0, keepdims=True)
    totals = jnp.where(in_passages[0:1], totals, 1.0)
    labels = labels_ref[...].astype(F32)
    label_col = jnp.sum(jnp.where(eye, jnp.broadcast_to(labels, (32, 32)), 0.0), axis=1, keepdims=True)
    row_id = iota((32, TAG), 0)
    label_row = jnp.sum(
        jnp.where(wide - 32 == row_id, jnp.broadcast_to(label_col, (32, TAG)), 0.0), axis=0, keepdims=True
    )
    chosen = jnp.where((row_id.astype(F32) == label_row) & in_passages, 1.0, 0.0)
    per_passage = jnp.log(totals) - jnp.sum(chosen * scores, axis=0, keepdims=True)
    loss_ref[...] = jnp.sum(per_passage, axis=1, keepdims=True) / 32.0
    score_grad = (loss_scale * score_scale / 32.0) * (exp_scores / totals - chosen)
    blank = jnp.zeros((TAG - 32, TAG), F32)
    grad_full = jnp.concatenate([score_grad, blank], axis=0)
    cos_full = jnp.concatenate([cosine, blank], axis=0)
    grad_sym = grad_full + jnp.transpose(grad_full)
    cos_sym = cos_full + jnp.transpose(cos_full)
    radial = jnp.sum(grad_sym * cos_sym, axis=1, keepdims=True)
    inv_norm = 1.0 / norm_col
    unit = pooled * inv_norm
    pooled_grad = (dot(grad_sym, unit, precision=precise) - unit * radial) * inv_norm
    sum_grad = pooled_grad * inv_count / (4.0 * (1.0 + pooled_sum))

    thirds = jnp.concatenate(split3(sum_grad), axis=0)
    new, old = iota((128, 128), 0), iota((128, 128), 1)
    source = (new // 32) * 32 + ((new // 2) % 8) * 4 + ((new // 16) % 2) * 2 + new % 2
    shuffle = jnp.where(source == old, 1.0, 0.0).astype(BF16)
    lg_swaps = []
    for i in range(4):
        rows = pl.ds(i * 128, 128)
        g = (dot(mt[rows, :], thirds) * fac[rows, :]).astype(BF16)
        lg[rows, :] = g
        p = dot(shuffle, g).astype(BF16)
        cx, part_of = i % 2, pl.ds((i // 2) * 16, 16)
        for b in range(8):
            lgp[cx * 2 + b % 2, b // 2, part_of] = p[b * 16 : b * 16 + 16]
        box = (pl.ds(cx * 2, 2), slice(None), part_of)
        swap = remote(lgp.at[box], lgs.at[box], e_send.at[1 + i], e_recv.at[1 + i], to_sib)
        launch(swap)
        lg_swaps.append(swap)

    span = half // 2
    side = span // 2

    def ring(o):
        return place((x + (1 - core) * o) % 4, (y + core * o) % 4, core, z)

    def ring_two(o):
        return place((x + core * o) % 4, (y + (1 - core) * o) % 4, core, z)

    def rows_of(ref, o):
        picked = []
        for i in range(4):
            px = (1 - core) * ((x + o) % 4) + core * i
            py = core * ((y + o) % 4) + (1 - core) * i
            picked.append(ref[px, py])
        return jnp.concatenate(picked, axis=0)

    def columns(n):
        return pl.ds(n * side, side)

    def term(rows, weights):
        return dot(rows, weights, ((1,), (1,)))

    def keep(o, n, value):
        part[o, :, :, columns(n)] = value.astype(BF16).reshape(4, 32, side)

    def partial(o, n, mine, theirs):
        keep(o, n, term(mine, w[core, columns(n), :]) + term(theirs, wsib[columns(n), :]))

    plus, minus = ring(1), ring(3)
    mine = rows_of(lgp, 2)
    for n in range(4):
        pre[:, columns(n)] = term(mine, w[core, columns(n), :])
    w_swap.wait_recv()
    for swap in lg_swaps:
        swap.wait_recv()
    theirs = rows_of(lgs, 2)
    fars = []
    for n in range(4):
        keep(2, n, pre[:, columns(n)] + term(theirs, wsib[columns(n), :]))
        copy = remote(part.at[2, :, :, columns(n)], fars_in.at[n], r_send.at[n], r_recv.at[n], (plus, minus)[n % 2])
        launch(copy)
        fars.append(copy)
    mine_up, theirs_up = rows_of(lgp, 1), rows_of(lgs, 1)
    mine_down, theirs_down = rows_of(lgp, 3), rows_of(lgs, 3)
    firsts = []

    def pass_on(o, n, k):
        target, landing = ((plus, fromm) if o == 1 else (minus, fromp))
        copy = remote(part.at[o, :, :, columns(n)], landing.at[n], r_send.at[k], r_recv.at[k], target)
        launch(copy)
        firsts.append(copy)

    for h in range(2):
        left, right = 2 * h, 2 * h + 1
        partial(1, right, mine_up, theirs_up)
        pass_on(1, right, 4 + right)
        partial(3, left, mine_down, theirs_down)
        pass_on(3, left, 4 + left)
        partial(1, left, mine_up, theirs_up)
        partial(3, right, mine_down, theirs_down)
        for n, o in ((left, 1), (right, 3)):
            fars[n].wait_recv()
            value = part[o, :, :, columns(n)].astype(F32) + fars_in[n].astype(F32)
            part[o, :, :, columns(n)] = value.astype(BF16)
            pass_on(o, n, 8 + n)
    mine, theirs = rows_of(lgp, 0), rows_of(lgs, 0)
    for n in range(4):
        partial(0, n, mine, theirs)

    def weight_step(i, carry):
        start = pl.multiple_of((i % per_quad) * deep, deep)
        a = hid[:, :, i // per_quad, :, pl.ds(start, deep)].reshape(tokens, deep)
        wgrad_ref[pl.ds(pl.multiple_of(i * deep, deep), deep), :] = dot(a, lg[...], ((0,), (0,))).astype(BF16)
        return carry

    seat = core * x + (1 - core) * y
    seconds = []
    for h in range(2):
        lax.fori_loop(h * per_half, (h + 1) * per_half, weight_step, 0)
        for copy in firsts[4 * h : 4 * h + 4]:
            copy.wait_recv()
        for o in (2, 1, 3, 0):
            i = (seat + o) % 4
            for n in (2 * h, 2 * h + 1):
                cols = columns(n)
                value = part[0, i, :, cols].astype(F32) + fromm[n, i].astype(F32) + fromp[n, i].astype(F32)
                acc[h, i, :, pl.ds((n % 2) * side, side)] = value.astype(BF16)
            if o:
                k = h * 3 + o - 1
                copy = remote(acc.at[h, i], rtwo.at[k], s_send.at[k], s_recv.at[k], ring_two(o))
                launch(copy)
                seconds.append(copy)
    wg_copy = pltpu.make_async_copy(wgrad_ref, wgrad_hbm, loc_sem.at[10])
    wg_copy.start()

    slab = span // 8
    new, old = iota((256, 256), 0), iota((256, 256), 1)
    source = (new % 8) * 32 + (new // 16) * 2 + (new // 8) % 2
    shuffle = jnp.where(source == old, 1.0, 0.0).astype(BF16)
    lasts = []
    for h in range(2):
        for copy in seconds[3 * h : 3 * h + 3]:
            copy.wait_recv()
        rows = acc[h, seat].astype(F32)
        for o in range(3):
            rows = rows + rtwo[h * 3 + o].astype(F32)
        rows = rows.astype(BF16)
        stacked = jnp.concatenate([rows[:, b * slab : (b + 1) * slab] for b in range(8)], axis=0)
        zsend[h] = dot(shuffle, stacked).astype(BF16).reshape(16, 16, slab)
        for k in range(1, PAIR):
            target = ((core + k // DEPTH) % 2) * DEPTH + (z + k % DEPTH) % DEPTH
            sem = h * PAIR + k
            copy = remote(zsend.at[h, target], zrecv.at[h, slot], z_send.at[sem], z_recv.at[sem], column_mate(k))
            launch(copy)
            lasts.append(copy)
        zrecv[h, slot] = zsend[h, slot]
    for h in range(2):
        for copy in lasts[15 * h : 15 * h + 15]:
            copy.wait_recv()
        for c in range(2):
            value = zrecv[h, c * DEPTH].astype(F32)
            for k in range(1, DEPTH):
                value = value + zrecv[h, c * DEPTH + k].astype(F32)
            for r in range(2):
                for b in range(8):
                    cols = pl.ds(c * half + h * span + b * slab, slab)
                    hgrad_ref[r : r + 1, cols] = value[r * 8 + b : r * 8 + b + 1]

    wg_copy.wait()
    for copy in sent:
        copy.wait_send()


def finish(loss_in, wgrad_in, hgrad_in, loss_out, wgrad_out, hgrad_out, loss, wgrad, hgrad, load_sem, store_sem):
    step = wgrad.shape[0] // CHUNKS
    stages = [(hgrad_in, hgrad, hgrad_out), (loss_in, loss, loss_out)]
    for i in range(CHUNKS):
        rows = pl.ds(i * step, step)
        stages.append((wgrad_in.at[rows, :], wgrad.at[rows, :], wgrad_out.at[rows, :]))
    loads = [pltpu.make_async_copy(src, via, load_sem.at[i]) for i, (src, via, _) in enumerate(stages)]
    stores = [pltpu.make_async_copy(via, dst, store_sem.at[i]) for i, (_, via, dst) in enumerate(stages)]
    for copy in loads:
        copy.start()
    for load, store in zip(loads, stores):
        load.wait()
        store.start()
    for copy in stores:
        copy.wait()


def body(hidden, head_weight, vocab_bias, seq_ids, token_mask, labels):
    width, voc = head_weight.shape
    half = width // 2
    tokens = GROUPS * TOK
    vmem = pl.BlockSpec(memory_space=pltpu.VMEM)
    hbm = pl.BlockSpec(memory_space=pltpu.HBM)
    dma = pltpu.SemaphoreType.DMA
    shapes = (
        jax.ShapeDtypeStruct((1, 1), F32),
        jax.ShapeDtypeStruct((width, voc), BF16),
        jax.ShapeDtypeStruct((2, width), F32),
    )
    results = pl.pallas_call(
        fused,
        out_shape=shapes,
        in_specs=[hbm] * 6,
        out_specs=(vmem, hbm, vmem),
        scratch_shapes=[
            pltpu.VMEM((voc // TAG, TAG), F32),
            pltpu.VMEM((1, TOK), jnp.int32),
            pltpu.VMEM((1, TOK), jnp.int32),
            pltpu.VMEM((1, 32), jnp.int32),
            pltpu.VMEM((width, voc), BF16),
            pltpu.VMEM((2, GROUPS // 2, 4, TOK, width // 4), BF16),
            pltpu.VMEM((2, GROUPS // 2, TOK, TAG), BF16),
            pltpu.VMEM((2, half, voc), BF16),
            pltpu.VMEM((half, voc), BF16),
            pltpu.VMEM((tokens, voc), F32),
            pltpu.VMEM((tokens, voc), F32),
            pltpu.VMEM((tokens, voc), F32),
            pltpu.VMEM((tokens, 3 * TAG), BF16),
            pltpu.VMEM((tokens, voc), BF16),
            pltpu.VMEM((4, 4, TOK, voc), BF16),
            pltpu.VMEM((4, 4, TOK, voc), BF16),
            pltpu.VMEM((PAIR, 16, TAG), F32),
            pltpu.VMEM((PAIR, 16, TAG), F32),
            pltpu.VMEM((4 * TOK, half), F32),
            pltpu.VMEM((4, 4, TOK, half), BF16),
            pltpu.VMEM((4, 4, TOK, half // 4), BF16),
            pltpu.VMEM((4, 4, TOK, half // 4), BF16),
            pltpu.VMEM((4, 4, TOK, half // 4), BF16),
            pltpu.VMEM((2, 4, TOK, half // 2), BF16),
            pltpu.VMEM((6, TOK, half // 2), BF16),
            pltpu.VMEM((2, PAIR, 16, half // 16), BF16),
            pltpu.VMEM((2, PAIR, 16, half // 16), BF16),
            dma((11,)),
            dma((GATHER_COPIES,)),
            dma((32,)),
            dma((32,)),
            dma((32,)),
            dma((8,)),
            dma((8,)),
            dma((5,)),
            dma((5,)),
            dma((PAIR,)),
            dma((PAIR,)),
            dma((PAIR,)),
            dma((PAIR,)),
            dma((12,)),
            dma((12,)),
            dma((6,)),
            dma((6,)),
            dma((2 * PAIR,)),
            dma((2 * PAIR,)),
        ],
        compiler_params=pltpu.CompilerParams(
            collective_id=0, has_side_effects=True, vmem_limit_bytes=60 * 1024 * 1024
        ),
        name="splade_head",
    )(
        hidden,
        head_weight,
        vocab_bias.reshape(voc // TAG, TAG),
        seq_ids,
        token_mask,
        labels.reshape(1, labels.shape[0]),
    )
    loss, weight_grad, hidden_grad = pl.pallas_call(
        finish,
        out_shape=shapes,
        in_specs=[hbm] * 3,
        out_specs=(hbm,) * 3,
        scratch_shapes=[
            *(pltpu.VMEM(shape.shape, shape.dtype) for shape in shapes),
            dma((CHUNKS + 2,)),
            dma((CHUNKS + 2,)),
        ],
        compiler_params=pltpu.CompilerParams(vmem_limit_bytes=60 * 1024 * 1024),
        name="results",
    )(*results)
    return loss.reshape(()), weight_grad, hidden_grad


def solution(mesh):
    in_specs = (
        P("dp", None),
        P(None, ("dp", "vocab")),
        P(("dp", "vocab")),
        P("dp", None),
        P("dp", None),
        P(),
    )
    out_specs = (P(), P(None, ("dp", "vocab")), P(("dp", "vocab"), None))
    return jax.shard_map(body, mesh=mesh, in_specs=in_specs, out_specs=out_specs, check_vma=False)
```

time: 82.8 us -> 73.2 us (0.88)
  local copies, waits for them, and re-layouts: 3.91 us -> 0 us
  Pallas kernels: 75 us -> 72.4 us
  between operations: 2.41 us -> 0.64 us
  other arithmetic: 1.35 us -> 0 us
    unnamed x4 -> x0, local copies, waits for them, and re-layouts: 3.22 us -> none
    pallas_call x1 -> x2, Pallas kernels: 75 us -> 72.4 us  [the longest x1 69 us: body(): pl.pallas_call(fused, out_shape=shapes, in_specs=[hbm] * 6, out_specs=(vm...]
where the time goes in v3:
time: 73.2 us; the launch traced here: 73.1 us
  Pallas kernels  72.4 us (99%)
    pallas_call x1, Pallas kernels, body(): pl.pallas_call(fused, out_shape=shapes, in_specs=[hbm] * 6, out_specs=(vm...  69 us
    pallas_call x1, Pallas kernels, body(): pl.pallas_call(finish, out_shape=shapes, in_specs=[hbm] * 3, out_specs=(h...  3.39 us

profile of v3, /device:TPU:1, one launch (start us, length us, event | category | flops | bytes accessed | tf_op | source)
XLA Modules:
  0.0 73.1 jit_solution(9174590308242817919)
XLA Ops:
  0.6 69.0 %splade_head.1 = (f32[1,1]{1,0:T(1,128)}, bf16[4096,384]{1,0:T(8,128)(2,1)}, f32[2,4096]{1,0:T(2,128)}) custom-call(bf16[32,4096]{1,0:T(8,128)(2,1)} %hidden_ref.1, bf16[4096,384]{1,0:T(8,128)(2,1)} %weight_ref.1, f32[3,128]{1,0:T(4,128)} %bitcast.3, s32[1,32]{1,0:T(1,128)} %seq_hbm.1, s32[1,32]{1,0:T(1,128)} %mask_hbm.1, s32[1,32]{1,0:T(1,128)} %bitcast.4), custom_call_target="tpu_custom_call" | custom-call | tf_op jit(solution)/shard_map/splade_head/pallas_call | solution.py:522
  69.7 3.4 %results.1 = (f32[1,1]{1,0:T(1,128)}, bf16[4096,384]{1,0:T(8,128)(2,1)}, f32[2,4096]{1,0:T(2,128)}) custom-call(f32[1,1]{1,0:T(1,128)} %get-tuple-element.9.loss_in, bf16[4096,384]{1,0:T(8,128)(2,1)} %get-tuple-element.10.wgrad_in, f32[2,4096]{1,0:T(2,128)} %get-tuple-element.11.hgrad_in), custom_call_target="tpu_custom_call" | custom-call | tf_op jit(solution)/shard_map/results/pallas_call | solution.py:587

commit v4 on v3

--- a/solution.py
+++ b/solution.py
@@ -22,7 +22,6 @@
 norm_eps = 1e-06
 precise = lax.Precision.HIGHEST
 
-GATHER_COPIES = 28
 PAIR = 16
 CHUNKS = 8
 
@@ -45,10 +44,10 @@
 
 def fused(
     hidden_ref, weight_ref, bias_hbm, seq_hbm, mask_hbm, labels_hbm,
-    loss_ref, wgrad_hbm, hgrad_ref,
-    bias_ref, seq_ref, mask_ref, labels_ref, wgrad_ref,
+    loss_hbm, wgrad_hbm, hgrad_hbm,
+    loss_ref, hgrad_ref, bias_ref, seq_ref, mask_ref, labels_ref, wgrad_ref,
     hid, tags_ref, w, wsib, logit, fac, excess, mt, lg, lgp, lgs,
-    ara, arb, pre, part, fars_in, fromm, fromp, acc, rtwo, zsend, zrecv,
+    pooled_six, sum_scale, ara, arb, pre, part, fars_in, fromm, fromp, acc, rtwo, zsend, zrecv,
     loc_sem, g_send, g_recv, h_send, h_recv, t_send, t_recv, e_send, e_recv, a_send, a_recv, b_send, b_recv,
     r_send, r_recv, s_send, s_recv, z_send, z_recv,
 ):
@@ -74,11 +73,13 @@
             src_ref=src, dst_ref=dst, send_sem=send, recv_sem=recv, device_id=device, device_id_type=MESH
         )
 
-    sent = []
-
-    def launch(copy):
-        copy.start()
-        sent.append(copy)
+    def all_sent(source, sem):
+        remote(source, source, sem, sem, to_sib).wait_send()
+
+    def all_here(target, sem):
+        remote(target, target, sem, sem, to_sib).wait_recv()
+
+    to_sib = place(x, y, 1 - core, z)
 
     w_copies = [
         pltpu.make_async_copy(weight_ref.at[pl.ds(h * half, half), :], w.at[h], loc_sem.at[h]) for h in range(2)
@@ -99,9 +100,14 @@
         copy.start()
 
     barrier = pltpu.get_barrier_semaphore()
-    for k in range(1, PAIR):
+    for k in (2, 1, 3):
+        pl.semaphore_signal(barrier, inc=1, device_id=plane_mate(k), device_id_type=MESH)
+    for k in (1, 7, 8):
         pl.semaphore_signal(barrier, inc=1, device_id=column_mate(k), device_id_type=MESH)
+    for k in range(4, PAIR):
         pl.semaphore_signal(barrier, inc=1, device_id=plane_mate(k), device_id_type=MESH)
+    for k in (2, 3, 4, 5, 6, 9, 10, 11, 12, 13, 14, 15):
+        pl.semaphore_signal(barrier, inc=1, device_id=column_mate(k), device_id_type=MESH)
 
     eye = iota((TOK, TOK), 0) == iota((TOK, TOK), 1)
     for copy in small_copies[:2]:
@@ -115,7 +121,6 @@
     other = 1 - xh
     cross_x = other * 2 + 1 - xl
     colour = (z + 2 * xl) % 4
-    to_sib = place(x, y, 1 - core, z)
     to_twin = place(xh * 2 + 1 - xl, y, core, z)
     to_above = place(x, y, core, (z + 1) % DEPTH)
     to_below = place(x, y, core, (z + DEPTH - 1) % DEPTH)
@@ -133,8 +138,6 @@
         (place(cross_x, up, core, z), 6, 2, (0,)),
         (place(cross_x, far, core, z), 7, 2, (0,)),
     )
-    free_sends = iter(range(GATHER_COPIES))
-
     def post(chunks, levels):
         for level in levels:
             for device, n, shift, quarters in fetches:
@@ -142,36 +145,36 @@
                     rq = quarters[level]
                     q = (colour + shift + rq) % 4
                     src = hid.at[core, seat_t, q]
-                    launch(remote(src, src, g_send.at[next(free_sends)], g_recv.at[n * 4 + rq], device))
+                    remote(src, src, g_send, g_recv.at[n * 4 + rq], device).start()
 
     for copy in h_copies:
         copy.wait()
     post((1, 2, 3, 4, 5, 6, 7), (0,))
     own_tags = tags_ref.at[core, seat_t]
     for device, n, _, _ in fetches:
-        launch(remote(own_tags, own_tags, t_send.at[n], t_recv.at[n], device))
+        remote(own_tags, own_tags, t_send.at[0], t_recv.at[n], device).start()
 
     def hand_over(n, rq):
         chunk = spot(n, rq)
-        launch(remote(chunk, chunk, h_send.at[n * 4 + rq], h_recv.at[n * 4 + rq], to_sib))
+        remote(chunk, chunk, h_send, h_recv.at[n], to_sib).start()
 
     def arrived(n, rq):
         chunk = spot(n, rq)
-        remote(chunk, chunk, g_send.at[0], g_recv.at[n * 4 + rq], to_sib).wait_recv()
+        all_here(chunk, g_recv.at[n * 4 + rq])
 
     for rq in range(4):
         hand_over(0, rq)
     for copy in w_copies + small_copies[2:]:
         copy.wait()
     w_swap = remote(w.at[1 - core], wsib, e_send.at[0], e_recv.at[0], to_sib)
-    launch(w_swap)
+    w_swap.start()
 
     for n in (4, 1, 2, 3, 5, 6, 7):
         arrived(n, 0)
         chunk = spot(n, 0)
         for device, rq, skipped in ((to_twin, 2, (1, 2)), (to_above, 3, (2, 4)), (to_below, 1, (1, 4))):
             if n not in skipped:
-                launch(remote(chunk, chunk, g_send.at[next(free_sends)], g_recv.at[n * 4 + rq], device))
+                remote(chunk, chunk, g_send, g_recv.at[n * 4 + rq], device).start()
         if n == 4:
             post((1, 2, 4), (1,))
         if n == 3:
@@ -179,41 +182,57 @@
         hand_over(n, 0)
     for n in range(1, 8):
         there = tags_ref.at[core, (xh if n < 4 else other) * 4 + (y, up, down, far)[n % 4]]
-        remote(there, there, t_send.at[n], t_recv.at[n], to_sib).wait_recv()
-    launch(remote(tags_ref.at[core], tags_ref.at[core], t_send.at[0], t_recv.at[0], to_sib))
-    for n in (4, 1, 2, 3, 5, 6, 7):
-        for rq in (2, 3, 1):
-            arrived(n, rq)
-            hand_over(n, rq)
-
+        all_here(there, t_recv.at[n])
+    remote(tags_ref.at[core], tags_ref.at[core], t_send.at[1], t_recv.at[0], to_sib).start()
     tokens = GROUPS * TOK
     deep = min(512, quad)
     per_half = half // deep
     per_quad = quad // deep
-
     share = tokens // 2
 
-    def logits_of(c):
-        rows = pl.ds(pl.multiple_of(c * share, share), share)
+    def logits_of(c, rows_x):
+        rows = pl.ds(pl.multiple_of(c * share + rows_x * 128, 128), 128)
         for b in range(voc // TAG):
-            logit[rows, pl.ds(b * TAG, TAG)] = jnp.broadcast_to(bias_ref[b : b + 1, :], (share, TAG))
+            logit[rows, pl.ds(b * TAG, TAG)] = jnp.broadcast_to(bias_ref[b : b + 1, :], (128, TAG))
 
         def step(q, carry):
-            a = hid[c, :, q].reshape(share, quad)
+            a = hid[c, pl.ds(rows_x * 4, 4), q].reshape(128, quad)
             logit[rows, :] += dot(a, w[q // 2, pl.ds(pl.multiple_of((q % 2) * quad, quad), quad), :])
             return carry
 
         lax.fori_loop(0, 4, step, 0)
 
-    logits_of(core)
-
-    remote(tags_ref.at[1 - core], tags_ref.at[1 - core], t_send.at[0], t_recv.at[0], to_sib).wait_recv()
-    for n in range(8):
-        for rq in range(4):
-            chunk = spot(n, rq, 1 - core)
-            remote(chunk, chunk, h_send.at[0], h_recv.at[n * 4 + rq], to_sib).wait_recv()
-
-    logits_of(1 - core)
+        def excess_step(i, carry):
+            rows = pl.ds(pl.multiple_of(c * share + rows_x * 128 + i * TOK, TOK), TOK)
+            l = logit[rows, :]
+            soft = jnp.maximum(l, 0.0) + jnp.log1p(jnp.exp(-jnp.abs(l)))
+            u = 1.0 + jnp.log1p(soft)
+            u2 = u * u
+            excess[rows, :] = u2 * u2 - 1.0
+            return carry
+
+        lax.fori_loop(0, 4, excess_step, 0)
+
+    def complete(chunks):
+        for n in chunks:
+            for rq in (2, 3, 1):
+                arrived(n, rq)
+                hand_over(n, rq)
+
+    def handed(chunks):
+        for n in chunks:
+            row = (xh if n < 4 else other) * 4 + (y, up, down, far)[n % 4]
+            all_here(hid.at[1 - core, row], h_recv.at[n])
+
+    complete((1, 2, 3))
+    logits_of(core, xh)
+    complete((4, 5, 6, 7))
+    logits_of(core, other)
+    handed((0, 1, 2, 3))
+    logits_of(1 - core, xh)
+    handed((4, 5, 6, 7))
+    logits_of(1 - core, other)
+    all_here(tags_ref.at[1 - core], t_recv.at[0])
 
     tags = tags_ref[...].reshape(tokens, TAG).astype(F32)
     row = iota((tokens, TAG), 0)
@@ -234,19 +253,13 @@
     inv_count = 1.0 / jnp.maximum(jnp.sum(member, axis=1, keepdims=True), 1.0)
     member = member.astype(BF16)
 
-    def excess_step(i, carry):
-        rows = pl.ds(pl.multiple_of(i * TOK, TOK), TOK)
-        l = logit[rows, :]
-        soft = jnp.maximum(l, 0.0) + jnp.log1p(jnp.exp(-jnp.abs(l)))
-        u = 1.0 + jnp.log1p(soft)
-        u2 = u * u
-        excess[rows, :] = u2 * u2 - 1.0
-        return carry
-
-    lax.fori_loop(0, GROUPS, excess_step, 0)
     e1, e2, e3 = split3(excess[...])
     pooled_sum = (dot(member, e1) + dot(member, e2) + dot(member, e3)) * inv_count
     pooled = jnp.log1p(pooled_sum) * 0.25
+    p1, p2, p3 = split3(pooled)
+    for i, piece in enumerate((p1, p2, p1, p3, p2, p1)):
+        pooled_six[pl.ds(i * TAG, TAG), :] = piece
+    sum_scale[...] = inv_count / (4.0 * (1.0 + pooled_sum))
 
     wide = iota((32, TAG), 1)
     in_passages = (wide >= 32) & (wide < 64)
@@ -264,12 +277,9 @@
     ara[slot, 0:8, :] = packed
     ara[slot, 8:9, :] = squares[0:1]
     message = pl.ds(0, 9)
-    a_copies = [
-        remote(ara.at[slot, message], ara.at[slot, message], a_send.at[k], a_recv.at[k], column_mate(k))
-        for k in range(1, PAIR)
-    ]
-    for copy in a_copies:
-        launch(copy)
+    mail = ara.at[slot, message]
+    for k in range(1, PAIR):
+        remote(mail, mail, a_send, a_recv, column_mate(k)).start()
 
     def factor_step(i, carry):
         rows = pl.ds(pl.multiple_of(i * TOK, TOK), TOK)
@@ -283,21 +293,21 @@
 
     lax.fori_loop(0, GROUPS, factor_step, 0)
 
-    for copy in a_copies:
-        copy.wait_recv()
+    all_here(ara.at[pl.ds(1, PAIR - 1), message], a_recv)
     column_sum = ara[0, message]
     for k in range(1, PAIR):
         column_sum = column_sum + ara[k, message]
     slot_b = x * SIDE + y
     arb[slot_b, message] = column_sum
-    b_copies = [
-        remote(arb.at[slot_b, message], arb.at[slot_b, message], b_send.at[k], b_recv.at[k], plane_mate(k))
-        for k in range(1, PAIR)
-    ]
-    for copy in b_copies:
-        launch(copy)
-    for copy in b_copies:
-        copy.wait_recv()
+    mail = arb.at[slot_b, message]
+    for k in range(1, PAIR):
+        remote(mail, mail, b_send, b_recv, plane_mate(k)).start()
+    all_sent(hid.at[0, pl.ds(0, 7)], g_send)
+    all_sent(hid.at[0], h_send)
+    all_sent(tags_ref.at[0, pl.ds(0, 7)], t_send.at[0])
+    all_sent(tags_ref.at[0], t_send.at[1])
+    all_sent(ara.at[pl.ds(1, PAIR - 1), message], a_send)
+    all_here(arb.at[pl.ds(1, PAIR - 1), message], b_recv)
     total = arb[0, message]
     for k in range(1, PAIR):
         total = total + arb[k, message]
@@ -325,7 +335,6 @@
     )
     chosen = jnp.where((row_id.astype(F32) == label_row) & in_passages, 1.0, 0.0)
     per_passage = jnp.log(totals) - jnp.sum(chosen * scores, axis=0, keepdims=True)
-    loss_ref[...] = jnp.sum(per_passage, axis=1, keepdims=True) / 32.0
     score_grad = (loss_scale * score_scale / 32.0) * (exp_scores / totals - chosen)
     blank = jnp.zeros((TAG - 32, TAG), F32)
     grad_full = jnp.concatenate([score_grad, blank], axis=0)
@@ -333,10 +342,10 @@
     grad_sym = grad_full + jnp.transpose(grad_full)
     cos_sym = cos_full + jnp.transpose(cos_full)
     radial = jnp.sum(grad_sym * cos_sym, axis=1, keepdims=True)
-    inv_norm = 1.0 / norm_col
-    unit = pooled * inv_norm
-    pooled_grad = (dot(grad_sym, unit, precision=precise) - unit * radial) * inv_norm
-    sum_grad = pooled_grad * inv_count / (4.0 * (1.0 + pooled_sum))
+    inv_col, inv_row = 1.0 / norm_col, 1.0 / norm_row
+    mix = inv_col * (grad_sym * inv_row - jnp.where(eye_wide, radial * inv_col, 0.0))
+    m1, m2, m3 = split3(mix)
+    sum_grad = dot(jnp.concatenate([m1, m1, m2, m1, m2, m3], axis=1), pooled_six[...]) * sum_scale[...]
 
     thirds = jnp.concatenate(split3(sum_grad), axis=0)
     new, old = iota((128, 128), 0), iota((128, 128), 1)
@@ -353,8 +362,10 @@
             lgp[cx * 2 + b % 2, b // 2, part_of] = p[b * 16 : b * 16 + 16]
         box = (pl.ds(cx * 2, 2), slice(None), part_of)
         swap = remote(lgp.at[box], lgs.at[box], e_send.at[1 + i], e_recv.at[1 + i], to_sib)
-        launch(swap)
+        swap.start()
         lg_swaps.append(swap)
+
+    loss_ref[...] = jnp.sum(per_passage, axis=1, keepdims=True) / 32.0
 
     span = half // 2
     side = span // 2
@@ -396,8 +407,8 @@
     fars = []
     for n in range(4):
         keep(2, n, pre[:, columns(n)] + term(theirs, wsib[columns(n), :]))
-        copy = remote(part.at[2, :, :, columns(n)], fars_in.at[n], r_send.at[n], r_recv.at[n], (plus, minus)[n % 2])
-        launch(copy)
+        copy = remote(part.at[2, :, :, columns(n)], fars_in.at[n], r_send, r_recv.at[n], (plus, minus)[n % 2])
+        copy.start()
         fars.append(copy)
     mine_up, theirs_up = rows_of(lgp, 1), rows_of(lgs, 1)
     mine_down, theirs_down = rows_of(lgp, 3), rows_of(lgs, 3)
@@ -405,8 +416,8 @@
 
     def pass_on(o, n, k):
         target, landing = ((plus, fromm) if o == 1 else (minus, fromp))
-        copy = remote(part.at[o, :, :, columns(n)], landing.at[n], r_send.at[k], r_recv.at[k], target)
-        launch(copy)
+        copy = remote(part.at[o, :, :, columns(n)], landing.at[n], r_send, r_recv.at[k], target)
+        copy.start()
         firsts.append(copy)
 
     for h in range(2):
@@ -433,7 +444,6 @@
         return carry
 
     seat = core * x + (1 - core) * y
-    seconds = []
     for h in range(2):
         lax.fori_loop(h * per_half, (h + 1) * per_half, weight_step, 0)
         for copy in firsts[4 * h : 4 * h + 4]:
@@ -446,20 +456,22 @@
                 acc[h, i, :, pl.ds((n % 2) * side, side)] = value.astype(BF16)
             if o:
                 k = h * 3 + o - 1
-                copy = remote(acc.at[h, i], rtwo.at[k], s_send.at[k], s_recv.at[k], ring_two(o))
-                launch(copy)
-                seconds.append(copy)
+                copy = remote(acc.at[h, i], rtwo.at[k], s_send, s_recv.at[h], ring_two(o))
+                copy.start()
     wg_copy = pltpu.make_async_copy(wgrad_ref, wgrad_hbm, loc_sem.at[10])
     wg_copy.start()
+    w_swap.wait_send()
+    for swap in lg_swaps:
+        swap.wait_send()
+    all_sent(arb.at[pl.ds(1, PAIR - 1), message], b_send)
+    all_sent(part.at[pl.ds(0, 3)], r_send)
 
     slab = span // 8
     new, old = iota((256, 256), 0), iota((256, 256), 1)
     source = (new % 8) * 32 + (new // 16) * 2 + (new // 8) % 2
     shuffle = jnp.where(source == old, 1.0, 0.0).astype(BF16)
-    lasts = []
     for h in range(2):
-        for copy in seconds[3 * h : 3 * h + 3]:
-            copy.wait_recv()
+        all_here(rtwo.at[pl.ds(3 * h, 3)], s_recv.at[h])
         rows = acc[h, seat].astype(F32)
         for o in range(3):
             rows = rows + rtwo[h * 3 + o].astype(F32)
@@ -468,14 +480,11 @@
         zsend[h] = dot(shuffle, stacked).astype(BF16).reshape(16, 16, slab)
         for k in range(1, PAIR):
             target = ((core + k // DEPTH) % 2) * DEPTH + (z + k % DEPTH) % DEPTH
-            sem = h * PAIR + k
-            copy = remote(zsend.at[h, target], zrecv.at[h, slot], z_send.at[sem], z_recv.at[sem], column_mate(k))
-            launch(copy)
-            lasts.append(copy)
+            remote(zsend.at[h, target], zrecv.at[h, slot], z_send, z_recv.at[h], column_mate(k)).start()
         zrecv[h, slot] = zsend[h, slot]
+    all_sent(rtwo, s_send)
     for h in range(2):
-        for copy in lasts[15 * h : 15 * h + 15]:
-            copy.wait_recv()
+        all_here(zrecv.at[h, pl.ds(1, PAIR - 1)], z_recv.at[h])
         for c in range(2):
             value = zrecv[h, c * DEPTH].astype(F32)
             for k in range(1, DEPTH):
@@ -485,9 +494,17 @@
                     cols = pl.ds(c * half + h * span + b * slab, slab)
                     hgrad_ref[r : r + 1, cols] = value[r * 8 + b : r * 8 + b + 1]
 
+    out_copies = [
+        pltpu.make_async_copy(hgrad_ref, hgrad_hbm, loc_sem.at[11]),
+        pltpu.make_async_copy(loss_ref, loss_hbm, loc_sem.at[12]),
+    ]
+    for copy in out_copies:
+        copy.start()
+    for h in range(2):
+        all_sent(zsend.at[h, pl.ds(1, PAIR - 1)], z_send)
+    for copy in out_copies:
+        copy.wait()
     wg_copy.wait()
-    for copy in sent:
-        copy.wait_send()
 
 
 def finish(loss_in, wgrad_in, hgrad_in, loss_out, wgrad_out, hgrad_out, loss, wgrad, hgrad, load_sem, store_sem):
@@ -511,7 +528,6 @@
     width, voc = head_weight.shape
     half = width // 2
     tokens = GROUPS * TOK
-    vmem = pl.BlockSpec(memory_space=pltpu.VMEM)
     hbm = pl.BlockSpec(memory_space=pltpu.HBM)
     dma = pltpu.SemaphoreType.DMA
     shapes = (
@@ -523,8 +539,10 @@
         fused,
         out_shape=shapes,
         in_specs=[hbm] * 6,
-        out_specs=(vmem, hbm, vmem),
+        out_specs=(hbm, hbm, hbm),
         scratch_shapes=[
+            pltpu.VMEM((1, 1), F32),
+            pltpu.VMEM((2, width), F32),
             pltpu.VMEM((voc // TAG, TAG), F32),
             pltpu.VMEM((1, TOK), jnp.int32),
             pltpu.VMEM((1, TOK), jnp.int32),
@@ -541,6 +559,8 @@
             pltpu.VMEM((tokens, voc), BF16),
             pltpu.VMEM((4, 4, TOK, voc), BF16),
             pltpu.VMEM((4, 4, TOK, voc), BF16),
+            pltpu.VMEM((6 * TAG, voc), BF16),
+            pltpu.VMEM((TAG, voc), F32),
             pltpu.VMEM((PAIR, 16, TAG), F32),
             pltpu.VMEM((PAIR, 16, TAG), F32),
             pltpu.VMEM((4 * TOK, half), F32),
@@ -552,25 +572,25 @@
             pltpu.VMEM((6, TOK, half // 2), BF16),
             pltpu.VMEM((2, PAIR, 16, half // 16), BF16),
             pltpu.VMEM((2, PAIR, 16, half // 16), BF16),
-            dma((11,)),
-            dma((GATHER_COPIES,)),
+            dma((13,)),
+            dma,
             dma((32,)),
-            dma((32,)),
-            dma((32,)),
+            dma,
             dma((8,)),
+            dma((2,)),
             dma((8,)),
             dma((5,)),
             dma((5,)),
-            dma((PAIR,)),
-            dma((PAIR,)),
-            dma((PAIR,)),
-            dma((PAIR,)),
+            dma,
+            dma,
+            dma,
+            dma,
+            dma,
             dma((12,)),
-            dma((12,)),
-            dma((6,)),
-            dma((6,)),
-            dma((2 * PAIR,)),
-            dma((2 * PAIR,)),
+            dma,
+            dma((2,)),
+            dma,
+            dma((2,)),
         ],
         compiler_params=pltpu.CompilerParams(
             collective_id=0, has_side_effects=True, vmem_limit_bytes=60 * 1024 * 1024

time: 73.2 us -> 71 us (0.970)
  Pallas kernels: 72.4 us -> 70.2 us
    pallas_call x1, Pallas kernels: 69 us -> 66.8 us  [body(): pl.pallas_call(fused, out_shape=shapes, in_specs=[hbm] * 6, out_specs=(hb...]
where the time goes in v4:
time: 71 us; the launch traced here: 70.9 us
  Pallas kernels  70.2 us (99%)
    pallas_call x1, Pallas kernels, body(): pl.pallas_call(fused, out_shape=shapes, in_specs=[hbm] * 6, out_specs=(hb...  66.8 us
    pallas_call x1, Pallas kernels, body(): pl.pallas_call(finish, out_shape=shapes, in_specs=[hbm] * 3, out_specs=(h...  3.39 us

profile of v4, /device:TPU:1, one launch (start us, length us, event | category | flops | bytes accessed | tf_op | source)
XLA Modules:
  0.0 70.9 jit_solution(5103207647291607712)
XLA Ops:
  0.6 66.8 %splade_head.1 = (f32[1,1]{1,0:T(1,128)}, bf16[4096,384]{1,0:T(8,128)(2,1)}, f32[2,4096]{1,0:T(2,128)}) custom-call(bf16[32,4096]{1,0:T(8,128)(2,1)} %hidden_ref.1, bf16[4096,384]{1,0:T(8,128)(2,1)} %weight_ref.1, f32[3,128]{1,0:T(4,128)} %bitcast.3, s32[1,32]{1,0:T(1,128)} %seq_hbm.1, s32[1,32]{1,0:T(1,128)} %mask_hbm.1, s32[1,32]{1,0:T(1,128)} %bitcast.4), custom_call_target="tpu_custom_call" | custom-call | tf_op jit(solution)/shard_map/splade_head/pallas_call | solution.py:538
  67.5 3.4 %results.1 = (f32[1,1]{1,0:T(1,128)}, bf16[4096,384]{1,0:T(8,128)(2,1)}, f32[2,4096]{1,0:T(2,128)}) custom-call(f32[1,1]{1,0:T(1,128)} %get-tuple-element.9.loss_in, bf16[4096,384]{1,0:T(8,128)(2,1)} %get-tuple-element.10.wgrad_in, f32[2,4096]{1,0:T(2,128)} %get-tuple-element.11.hgrad_in), custom_call_target="tpu_custom_call" | custom-call | tf_op jit(solution)/shard_map/results/pallas_call | solution.py:607

commit v5 on v4

--- a/solution.py
+++ b/solution.py
@@ -24,6 +24,8 @@
 
 PAIR = 16
 CHUNKS = 8
+COLUMN_ORDER = (12, 4, 11, 13, 3, 5, 10, 14, 2, 6, 9, 15, 1, 7, 8)
+PLANE_ORDER = (10, 9, 11, 6, 14, 2, 8, 5, 7, 13, 15, 1, 3, 4, 12)
 
 
 def iota(shape, dim):
@@ -190,20 +192,17 @@
     per_quad = quad // deep
     share = tokens // 2
 
-    def logits_of(c, rows_x):
-        rows = pl.ds(pl.multiple_of(c * share + rows_x * 128, 128), 128)
-        for b in range(voc // TAG):
-            logit[rows, pl.ds(b * TAG, TAG)] = jnp.broadcast_to(bias_ref[b : b + 1, :], (128, TAG))
-
-        def step(q, carry):
-            a = hid[c, pl.ds(rows_x * 4, 4), q].reshape(128, quad)
-            logit[rows, :] += dot(a, w[q // 2, pl.ds(pl.multiple_of((q % 2) * quad, quad), quad), :])
-            return carry
-
-        lax.fori_loop(0, 4, step, 0)
+    def logits_of(c):
+        rows = pl.ds(pl.multiple_of(c * share, share), share)
+        bias = jnp.concatenate([bias_ref[b : b + 1, :] for b in range(voc // TAG)], axis=1)
+        value = jnp.broadcast_to(bias, (share, voc))
+        for q in range(4):
+            a = hid[c, :, q].reshape(share, quad)
+            value = value + dot(a, w[q // 2, pl.ds((q % 2) * quad, quad), :])
+        logit[rows, :] = value
 
         def excess_step(i, carry):
-            rows = pl.ds(pl.multiple_of(c * share + rows_x * 128 + i * TOK, TOK), TOK)
+            rows = pl.ds(pl.multiple_of(c * share + i * 64, 64), 64)
             l = logit[rows, :]
             soft = jnp.maximum(l, 0.0) + jnp.log1p(jnp.exp(-jnp.abs(l)))
             u = 1.0 + jnp.log1p(soft)
@@ -224,14 +223,10 @@
             row = (xh if n < 4 else other) * 4 + (y, up, down, far)[n % 4]
             all_here(hid.at[1 - core, row], h_recv.at[n])
 
-    complete((1, 2, 3))
-    logits_of(core, xh)
-    complete((4, 5, 6, 7))
-    logits_of(core, other)
-    handed((0, 1, 2, 3))
-    logits_of(1 - core, xh)
-    handed((4, 5, 6, 7))
-    logits_of(1 - core, other)
+    complete((1, 2, 3, 4, 5, 6, 7))
+    logits_of(core)
+    handed((0, 1, 2, 3, 4, 5, 6, 7))
+    logits_of(1 - core)
     all_here(tags_ref.at[1 - core], t_recv.at[0])
 
     tags = tags_ref[...].reshape(tokens, TAG).astype(F32)
@@ -278,11 +273,11 @@
     ara[slot, 8:9, :] = squares[0:1]
     message = pl.ds(0, 9)
     mail = ara.at[slot, message]
-    for k in range(1, PAIR):
+    for k in COLUMN_ORDER:
         remote(mail, mail, a_send, a_recv, column_mate(k)).start()
 
     def factor_step(i, carry):
-        rows = pl.ds(pl.multiple_of(i * TOK, TOK), TOK)
+        rows = pl.ds(pl.multiple_of(i * 64, 64), 64)
         l = logit[rows, :]
         e = jnp.exp(-jnp.abs(l))
         soft = jnp.maximum(l, 0.0) + jnp.log1p(e)
@@ -291,7 +286,7 @@
         fac[rows, :] = 4.0 * (u * u * u) * top / ((1.0 + e) * (1.0 + soft))
         return carry
 
-    lax.fori_loop(0, GROUPS, factor_step, 0)
+    lax.fori_loop(0, GROUPS // 2, factor_step, 0)
 
     all_here(ara.at[pl.ds(1, PAIR - 1), message], a_recv)
     column_sum = ara[0, message]
@@ -300,7 +295,7 @@
     slot_b = x * SIDE + y
     arb[slot_b, message] = column_sum
     mail = arb.at[slot_b, message]
-    for k in range(1, PAIR):
+    for k in PLANE_ORDER:
         remote(mail, mail, b_send, b_recv, plane_mate(k)).start()
     all_sent(hid.at[0, pl.ds(0, 7)], g_send)
     all_sent(hid.at[0], h_send)
@@ -478,7 +473,7 @@
         rows = rows.astype(BF16)
         stacked = jnp.concatenate([rows[:, b * slab : (b + 1) * slab] for b in range(8)], axis=0)
         zsend[h] = dot(shuffle, stacked).astype(BF16).reshape(16, 16, slab)
-        for k in range(1, PAIR):
+        for k in COLUMN_ORDER:
             target = ((core + k // DEPTH) % 2) * DEPTH + (z + k % DEPTH) % DEPTH
             remote(zsend.at[h, target], zrecv.at[h, slot], z_send, z_recv.at[h], column_mate(k)).start()
         zrecv[h, slot] = zsend[h, slot]

time: 71 us -> 68.8 us (0.969)
  Pallas kernels: 70.2 us -> 68.1 us
    pallas_call x1, Pallas kernels: 66.8 us -> 64.7 us  [body(): pl.pallas_call(fused, out_shape=shapes, in_specs=[hbm] * 6, out_specs=(hb...]
where the time goes in v5:
time: 68.8 us; the launch traced here: 68.7 us
  Pallas kernels  68.1 us (99%)
    pallas_call x1, Pallas kernels, body(): pl.pallas_call(fused, out_shape=shapes, in_specs=[hbm] * 6, out_specs=(hb...  64.7 us
    pallas_call x1, Pallas kernels, body(): pl.pallas_call(finish, out_shape=shapes, in_specs=[hbm] * 3, out_specs=(h...  3.39 us

profile of v5, /device:TPU:1, one launch (start us, length us, event | category | flops | bytes accessed | tf_op | source)
XLA Modules:
  0.0 68.7 jit_solution(702308814735826162)
XLA Ops:
  0.6 64.7 %splade_head.1 = (f32[1,1]{1,0:T(1,128)}, bf16[4096,384]{1,0:T(8,128)(2,1)}, f32[2,4096]{1,0:T(2,128)}) custom-call(bf16[32,4096]{1,0:T(8,128)(2,1)} %hidden_ref.1, bf16[4096,384]{1,0:T(8,128)(2,1)} %weight_ref.1, f32[3,128]{1,0:T(4,128)} %bitcast.3, s32[1,32]{1,0:T(1,128)} %seq_hbm.1, s32[1,32]{1,0:T(1,128)} %mask_hbm.1, s32[1,32]{1,0:T(1,128)} %bitcast.4), custom_call_target="tpu_custom_call" | custom-call | tf_op jit(solution)/shard_map/splade_head/pallas_call | solution.py:533
  65.3 3.4 %results.1 = (f32[1,1]{1,0:T(1,128)}, bf16[4096,384]{1,0:T(8,128)(2,1)}, f32[2,4096]{1,0:T(2,128)}) custom-call(f32[1,1]{1,0:T(1,128)} %get-tuple-element.9.loss_in, bf16[4096,384]{1,0:T(8,128)(2,1)} %get-tuple-element.10.wgrad_in, f32[2,4096]{1,0:T(2,128)} %get-tuple-element.11.hgrad_in), custom_call_target="tpu_custom_call" | custom-call | tf_op jit(solution)/shard_map/results/pallas_call | solution.py:602

commit v6 on v5

--- a/solution.py
+++ b/solution.py
@@ -389,7 +389,8 @@
         part[o, :, :, columns(n)] = value.astype(BF16).reshape(4, 32, side)
 
     def partial(o, n, mine, theirs):
-        keep(o, n, term(mine, w[core, columns(n), :]) + term(theirs, wsib[columns(n), :]))
+        weights = jnp.concatenate([w[core, columns(n), :], wsib[columns(n), :]], axis=1)
+        keep(o, n, term(jnp.concatenate([mine, theirs], axis=1), weights))
 
     plus, minus = ring(1), ring(3)
     mine = rows_of(lgp, 2)

time: 68.8 us -> 68.9 us (level)
  no operation moved by 1% of the time
where the time goes in v6:
time: 68.9 us; the launch traced here: 68.8 us
  Pallas kernels  68.2 us (99%)
    pallas_call x1, Pallas kernels, body(): pl.pallas_call(fused, out_shape=shapes, in_specs=[hbm] * 6, out_specs=(hb...  64.8 us
    pallas_call x1, Pallas kernels, body(): pl.pallas_call(finish, out_shape=shapes, in_specs=[hbm] * 3, out_specs=(h...  3.39 us

profile of v6, /device:TPU:1, one launch (start us, length us, event | category | flops | bytes accessed | tf_op | source)
XLA Modules:
  0.0 68.8 jit_solution(4746778916892126928)
XLA Ops:
  0.6 64.8 %splade_head.1 = (f32[1,1]{1,0:T(1,128)}, bf16[4096,384]{1,0:T(8,128)(2,1)}, f32[2,4096]{1,0:T(2,128)}) custom-call(bf16[32,4096]{1,0:T(8,128)(2,1)} %hidden_ref.1, bf16[4096,384]{1,0:T(8,128)(2,1)} %weight_ref.1, f32[3,128]{1,0:T(4,128)} %bitcast.3, s32[1,32]{1,0:T(1,128)} %seq_hbm.1, s32[1,32]{1,0:T(1,128)} %mask_hbm.1, s32[1,32]{1,0:T(1,128)} %bitcast.4), custom_call_target="tpu_custom_call" | custom-call | tf_op jit(solution)/shard_map/splade_head/pallas_call | solution.py:534
  65.4 3.4 %results.1 = (f32[1,1]{1,0:T(1,128)}, bf16[4096,384]{1,0:T(8,128)(2,1)}, f32[2,4096]{1,0:T(2,128)}) custom-call(f32[1,1]{1,0:T(1,128)} %get-tuple-element.9.loss_in, bf16[4096,384]{1,0:T(8,128)(2,1)} %get-tuple-element.10.wgrad_in, f32[2,4096]{1,0:T(2,128)} %get-tuple-element.11.hgrad_in), custom_call_target="tpu_custom_call" | custom-call | tf_op jit(solution)/shard_map/results/pallas_call | solution.py:603
